TPU v7x, 32 devices: a whole 2x2x4 slice. The times are simulated.
32 devices in a mesh: patch: 16 (over z, y, x), stream: 2 (over core).
Axes of the slice: x: 2, y: 2, z: 4, core: 2. Of those that a mesh axis runs over, the one named last changes fastest.
Arguments:
- exposures: bfloat16 [4, 2, 256, 8, 4096], P(None, 'stream', 'patch'), may hold values from -6 to 6
- owners: int32 [4, 2, 256, 2], P(None, 'stream', 'patch'), may hold values from 0 to 15, all different within a row; in each aligned block of 16 rows (0 to 15, 16 to 31, ..., all dimensions but the last counted through in order) at most 2 rows name the same one
- offsets: int32 [4, 2, 256, 2], P(None, 'stream', 'patch'), may hold values from 0 to 56
- visit_shift: float32 [4, 2, 2], P(None, 'stream'), may hold values from 0.05 to 0.95
- visit_weight: float32 [4, 2], P(None, 'stream'), may hold values from 0.25 to 4
- psf_class: int32 [4, 2], P(None, 'stream'), may hold values from 0 to 7
- coef_table: float32 [8, 16], replicated, may hold values from -0.18 to 0.18
- basis_x: float32 [16, 31], replicated, may hold values from -1 to 1
- basis_y: float32 [16, 31], replicated, may hold values from -1 to 1
Outputs:
- coadd: float32 [1024, 4096], P(('patch', 'stream'))
Inputs may be any that keep to these rules, and one draw needn't show every extreme that they name: `owners`: each row names 2 different patches; in each step the 16 strips of one holder name one patch at most 2 times, a bound that some block reaches.
All inputs are finite; a program needn't handle non-finite values.
Results may differ from a plain program's by a relative error of at most 0.0062.
Values may be sent and summed in bfloat16 or wider, within the bound.
A program may use at most 128 MiB of HBM per device.

v0:
```python
import functools

import jax
import jax.numpy as jnp
import numpy as np
from jax import lax
from jax.experimental import pallas as pl
from jax.experimental.pallas import tpu as pltpu
from jax.sharding import PartitionSpec as P

SLAB_ROWS = 64
ROWS = 8
TAPS_OUT = 36
CHUNKS = 4
SUB = 512
EMPTY = 128
VMEM_LIMIT = 58 * 1024 * 1024
HI = lax.Precision.HIGHEST


def lanczos_taps(fraction):
    distance = jnp.arange(6, dtype=jnp.int32).astype(jnp.float32) - 2.0 - fraction[..., None]
    values = jnp.sinc(distance) * jnp.sinc(distance / 3.0)
    return values / jnp.sum(values, axis=-1, keepdims=True)


def column_rows(basis_x, warp_x):
    summed = 0.0
    for q in range(6):
        part = basis_x[None, :, :] * warp_x[:, q, None, None]
        summed = summed + jnp.pad(part, ((0, 0), (0, 0), (q, 5 - q)))
    hx = summed.astype(jnp.bfloat16).astype(jnp.float32)
    return jnp.pad(hx[:, :, ::-1], ((0, 0), (0, 0), (206, 14)))


def row_table(weight, coeffs, basis_y, warp_y):
    steps, bases, taps = weight.shape[0], basis_y.shape[0], basis_y.shape[1]
    mix = basis_y[None] * (weight[:, None] * coeffs)[:, :, None]
    mix = mix.astype(jnp.bfloat16).astype(jnp.float32)
    i = np.arange(ROWS)
    tap = i[None, :] - i[:, None] + 2
    pick = (tap[:, :, None] == np.arange(6)).astype(np.float32)
    ymat = jnp.sum(pick[None] * warp_y[:, None, None, :], axis=3)
    ymat = ymat.astype(jnp.bfloat16).astype(jnp.float32)
    outer = mix.transpose(0, 2, 1)[:, :, None, :, None] * ymat[:, None, :, None, :]
    outer = outer.reshape(steps, taps * ROWS, bases * ROWS)
    u = np.arange(taps)
    place = (i[None, None, :] + 71 - u[None, :, None]) == np.arange(192)[:, None, None]
    place = place.astype(np.float32).reshape(192, taps * ROWS)
    return jnp.einsum("qk,tkn->tqn", place, outer, precision=HI)


def prep_kernel(streams, starts_ref, me_ref, v_ref, k2_ref, band_ref, w_ref):
    pairs = v_ref.shape[0] // 2
    patches = w_ref.shape[0]
    steps = k2_ref.shape[0]
    part = SLAB_ROWS // streams

    def one_band(g, c):
        for side in range(2):
            row = v_ref[pl.ds(g * 2 + side, 1), :]
            wide = jnp.broadcast_to(row, (256, 256))
            rolled = pltpu.roll(wide, 0, 1, stride=1, stride_axis=0)
            band_ref[g, :, side * 128 : (side + 1) * 128] = rolled[:, :128].astype(jnp.bfloat16)
        return c

    lax.fori_loop(0, pairs, one_band, 0)
    me = me_ref[0]

    def one_patch(q, c):
        for t in range(steps):
            for slot in range(2):
                base = starts_ref[(q * steps + t) * 2 + slot]
                rows = [
                    k2_ref[t, pl.ds(base + part * jnp.bitwise_xor(me, s), part), :]
                    for s in range(streams)
                ]
                block = jnp.concatenate(rows, axis=0).astype(jnp.bfloat16)
                w_ref[q, :, (t * 2 + slot) * 128 : (t * 2 + slot + 1) * 128] = block
        return c

    lax.fori_loop(0, patches, one_patch, 0)


def main_kernel(order, streams, strip_ref, x_ref, halo_ref, band_ref, w_ref, keep_ref, send_ref, f_ref):
    steps = x_ref.shape[0]
    strips = x_ref.shape[1] // ROWS
    patches = w_ref.shape[0]
    windows = SUB // 128
    part = SLAB_ROWS // streams

    for t in range(steps):
        pieces = []
        for n in range(windows):
            if n < windows - 1:
                pieces.append(x_ref[t, :, n * 128 : n * 128 + 256])
            else:
                pieces.append(jnp.concatenate([x_ref[t, :, n * 128 :], halo_ref[t]], axis=1))
        lhs = jnp.concatenate(pieces, axis=0)

        def one_pair(g, c):
            res = jnp.dot(lhs, band_ref[t * 8 + g], preferred_element_type=jnp.float32)
            res = res.reshape(windows, strips, ROWS, 256)
            for n in range(windows):
                two = jnp.concatenate([res[n, :, :, :128], res[n, :, :, 128:]], axis=1)
                f_ref[t * strips : (t + 1) * strips, g, :, n * 128 : (n + 1) * 128] = two.astype(jnp.bfloat16)
            return c

        lax.fori_loop(0, 8, one_pair, 0)

    bits = len(order)

    def one_patch(q, c):
        acc = jnp.zeros((SLAB_ROWS, SUB), jnp.float32)
        for t in range(steps):
            first = strip_ref[(q * steps + t) * 2]
            second = strip_ref[(q * steps + t) * 2 + 1]
            rhs = jnp.concatenate(
                [f_ref[first].reshape(128, SUB), f_ref[second].reshape(128, SUB)], axis=0
            )
            acc = acc + jnp.dot(
                w_ref[q, :, t * 256 : (t + 1) * 256], rhs, preferred_element_type=jnp.float32
            )
        pos = 0
        for place, bit in enumerate(order):
            pos = pos + (lax.shift_right_logical(q, bit) & 1) * (1 << (bits - 1 - place))
        for s in range(streams):
            rows = acc[s * part : (s + 1) * part]
            if s < streams // 2:
                keep_ref[s, pos] = rows
            else:
                send_ref[s - streams // 2, pos] = rows.astype(jnp.bfloat16)
        return c

    lax.fori_loop(0, patches, one_patch, 0)


def swap(x, axis, bit):
    n = lax.axis_size(axis)
    return lax.ppermute(x, axis, [(i, i ^ bit) for i in range(n)])


def shards(
    exposures, owners, offsets, visit_shift, visit_weight, psf_class, coef_table, basis_x, basis_y
):
    patches = lax.axis_size("patch")
    streams = lax.axis_size("stream")
    my_patch = lax.axis_index("patch")
    my_stream = lax.axis_index("stream")
    steps, strips, width = exposures.shape[0], exposures.shape[2], exposures.shape[4]
    part = SLAB_ROWS // streams
    patch_bits = patches.bit_length() - 1
    stream_bits = streams.bit_length() - 1

    x = exposures.reshape(steps, strips * ROWS, width)
    x = jnp.pad(x, ((0, 0), (0, 0), (32, 96)))

    warp = lanczos_taps(visit_shift[:, 0])
    vrows = column_rows(basis_x, warp[:, 0]).reshape(-1, 256)
    hits = (psf_class[:, 0, None] == jnp.arange(coef_table.shape[0], dtype=jnp.int32)).astype(jnp.float32)
    coeffs = jnp.sum(hits[:, :, None] * coef_table[None], axis=1)
    k2 = row_table(visit_weight[:, 0], coeffs, basis_y, warp[:, 1])

    wanted = jnp.bitwise_xor(jnp.arange(patches, dtype=jnp.int32), my_patch)
    own, off = owners[:, 0], offsets[:, 0]
    match = own[None] == wanted[:, None, None, None]
    named = jnp.any(match, axis=3)
    at = jnp.sum(jnp.where(match, off[None], 0), axis=3)
    ids = jnp.arange(strips, dtype=jnp.int32)
    first = jnp.min(jnp.where(named, ids, strips), axis=2)
    last = jnp.max(jnp.where(named, ids, -1), axis=2)
    one = named & (ids == first[..., None])
    two = named & (ids == last[..., None]) & (last > first)[..., None]
    start = jnp.stack(
        [jnp.sum(jnp.where(m, 56 - at - EMPTY, 0), axis=2) + EMPTY for m in (one, two)], axis=2
    )
    base = jnp.arange(steps, dtype=jnp.int32)[None] * strips
    strip = jnp.stack([base + jnp.clip(first, 0, strips - 1), base + jnp.clip(last, 0, strips - 1)], axis=2)
    start, strip = start.reshape(-1), strip.reshape(-1)

    smem = pl.BlockSpec(memory_space=pltpu.SMEM)
    vmem = pl.BlockSpec(memory_space=pltpu.VMEM)
    params = pltpu.CompilerParams(vmem_limit_bytes=VMEM_LIMIT)
    band, w = pl.pallas_call(
        functools.partial(prep_kernel, streams),
        out_shape=(
            jax.ShapeDtypeStruct((steps * 8, 256, 256), jnp.bfloat16),
            jax.ShapeDtypeStruct((patches, SLAB_ROWS, steps * 256), jnp.bfloat16),
        ),
        in_specs=[smem, smem, vmem, vmem],
        out_specs=(vmem, vmem),
        compiler_params=params,
    )(start, my_stream.reshape(1).astype(jnp.int32), vrows, k2)

    chunk = width // CHUNKS
    subs = chunk // SUB
    half = streams // 2
    flops = 2 * steps * strips * ROWS * chunk * 256 * 16 + 2 * patches * SLAB_ROWS * steps * 256 * chunk
    outs = []
    for c in range(CHUNKS):
        order = list(range(patch_bits))
        if c % 2 == 1:
            order[0], order[1] = order[1], order[0]
        first_sub = c * subs
        keep, send = pl.pallas_call(
            functools.partial(main_kernel, tuple(order), streams),
            grid_spec=pltpu.PrefetchScalarGridSpec(
                num_scalar_prefetch=1,
                grid=(subs,),
                in_specs=[
                    pl.BlockSpec((steps, strips * ROWS, SUB), lambda i, _, f=first_sub: (0, 0, f + i)),
                    pl.BlockSpec(
                        (steps, strips * ROWS, 128), lambda i, _, f=first_sub: (0, 0, (f + i + 1) * (SUB // 128))
                    ),
                    pl.BlockSpec(band.shape, lambda i, _: (0, 0, 0)),
                    pl.BlockSpec(w.shape, lambda i, _: (0, 0, 0)),
                ],
                out_specs=[
                    pl.BlockSpec((half, patches, part, SUB), lambda i, _: (0, 0, 0, i)),
                    pl.BlockSpec((half, patches, part, SUB), lambda i, _: (0, 0, 0, i)),
                ],
                scratch_shapes=[pltpu.VMEM((steps * strips, 8, 16, SUB), jnp.bfloat16)],
            ),
            out_shape=(
                jax.ShapeDtypeStruct((half, patches, part, chunk), jnp.float32),
                jax.ShapeDtypeStruct((half, patches, part, chunk), jnp.bfloat16),
            ),
            compiler_params=params,
            cost_estimate=pl.CostEstimate(flops=flops, bytes_accessed=12 << 20, transcendentals=0),
        )(strip, x, x, band, w)
        keep = keep.reshape(half * patches, part, chunk)
        send = send.reshape(half * patches, part, chunk)
        hops = [("stream", 1 << b) for b in reversed(range(stream_bits))]
        hops += [("patch", 1 << b) for b in order]
        for step, (axis, bit) in enumerate(hops):
            total = keep + swap(send, axis, bit).astype(jnp.float32)
            left = total.shape[0] // 2
            if step + 1 < len(hops):
                keep, send = total[:left], total[left:].astype(jnp.bfloat16)
        outs.append(total[0])
    return jnp.concatenate(outs, axis=1)


def solution(mesh):
    placed = (
        P(None, "stream", "patch", None, None),
        P(None, "stream", "patch", None),
        P(None, "stream", "patch", None),
        P(None, "stream", None),
        P(None, "stream"),
        P(None, "stream"),
        P(),
        P(),
        P(),
    )
    return jax.shard_map(
        shards, mesh=mesh, in_specs=placed, out_specs=P(("patch", "stream"), None), check_vma=False
    )
```

profile of v0, /device:TPU:0, one launch (start us, length us, event | category | flops | bytes accessed | tf_op | source)
XLA Modules:
  0.0 214.2 jit_solution(17049620325891335940)
XLA Ops:
  0.0 0.9 fusion.45
  0.9 0.3 slice_reduce_fusion.5
  1.1 0.8 broadcast_multiply_fusion.6
  1.9 0.1 fusion.9
  2.1 0.8 compare_reduce_fusion
  2.9 0.2 select_reduce_fusion.3
  3.1 0.8 fusion.4
  3.9 0.3 select_reduce_fusion.1
  4.2 0.1 copy.37
  4.4 0.6 reshape.213.starts_ref
  5.0 0.8 multiply_reduce_fusion
  5.8 0.8 copy.38
  6.6 0.7 fusion.48
  7.3 0.8 multiply_reduce_fusion.1
  8.1 0.7 broadcast_multiply_fusion.7
  8.8 3.7 %broadcast_multiply_fusion = f32[4,31,8,16,8]{4,3,2,1,0:T(8,128)} fusion(f32[4,8,8]{2,1,0:T(8,128)S(1)} %convert_element_type.205, f32[4,31,16]{2,1,0:T(8,128)S(1)} %fusion.5), kind=kLoop, calls=%fused_computation | loop fusion | flops 126976 | bytes 516864 | tf_op jit(solution)/shard_map/mul | solution.py:45
  12.6 6.2 %mul.249 = f32[4,248,128]{2,1,0:T(8,128)S(1)} reshape(f32[4,31,8,16,8]{4,3,2,1,0:T(8,128)} %broadcast_multiply_fusion) | data formatting | bytes 1015808 | tf_op jit(solution)/shard_map/mul | solution.py:45
  18.9 0.1 copy.34
  19.0 0.7 reshape.211.strip_ref
  19.7 0.7 pad.39
  20.4 1.3 convolution_bitcast_fusion.k2_ref
  21.7 6.9 %pad.32.x_ref.halo_ref = bf16[4,128,4224]{2,1,0:T(8,128)(2,1)} pad(bf16[4,128,4096]{2,1,0:T(8,128)(2,1)} %bitcast.48, bf16[]{:T(256)} %constant.65.clone.1), padding=0_0x0_0x32_96 | pad | bytes 8519682 | tf_op jit(solution)/shard_map/jit(_pad)/pad | solution.py:156
  28.6 7.6 %shard_map.115 = (bf16[32,256,256]{2,1,0:T(8,128)(2,1)}, bf16[16,64,1024]{2,1,0:T(8,128)(2,1)}) custom-call(s32[128]{0:T(128)} %reshape.213.starts_ref, s32[1]{0:T(128)} %bitcast.7.me_ref, f32[64,256]{1,0:T(8,128)} %bitcast.49, f32[4,192,128]{2,1,0:T(8,128)} %convolution_bitcast_fusion.k2_ref), custom_call_target="tpu_custom_call" | custom-call | tf_op jit(solution)/shard_map/pallas_call | solution.py:184
  36.1 29.5 %shard_map.116 = (f32[1,16,32,1024]{3,2,1,0:T(8,128)}, bf16[1,16,32,1024]{3,2,1,0:T(8,128)(2,1)}) custom-call(s32[128]{0:T(128)} %reshape.211.strip_ref, bf16[4,128,4224]{2,1,0:T(8,128)(2,1)} %pad.32.x_ref.halo_ref, bf16[4,128,4224]{2,1,0:T(8,128)(2,1)} %pad.32.x_ref.halo_ref, bf16[32,256,256]{2,1,0:T(8,128)(2,1)} %get-tuple-element.16.band_ref, ...), custom_call_target="tpu_custom_call" | custom-call | flops 6442450944 | bytes 12582912 | tf_op jit(solution)/shard_map/pallas_call | solution.py:205
  65.7 0.4 collective-permute-start
  66.1 29.5 %shard_map.117 = (f32[1,16,32,1024]{3,2,1,0:T(8,128)}, bf16[1,16,32,1024]{3,2,1,0:T(8,128)(2,1)}) custom-call(s32[128]{0:T(128)} %reshape.211.strip_ref, bf16[4,128,4224]{2,1,0:T(8,128)(2,1)} %pad.32.x_ref.halo_ref, bf16[4,128,4224]{2,1,0:T(8,128)(2,1)} %pad.32.x_ref.halo_ref, bf16[32,256,256]{2,1,0:T(8,128)(2,1)} %get-tuple-element.16.band_ref, ...), custom_call_target="tpu_custom_call" | custom-call | flops 6442450944 | bytes 12582912 | tf_op jit(solution)/shard_map/pallas_call | solution.py:205
  95.7 29.5 %shard_map.118 = (f32[1,16,32,1024]{3,2,1,0:T(8,128)}, bf16[1,16,32,1024]{3,2,1,0:T(8,128)(2,1)}) custom-call(s32[128]{0:T(128)} %reshape.211.strip_ref, bf16[4,128,4224]{2,1,0:T(8,128)(2,1)} %pad.32.x_ref.halo_ref, bf16[4,128,4224]{2,1,0:T(8,128)(2,1)} %pad.32.x_ref.halo_ref, bf16[32,256,256]{2,1,0:T(8,128)(2,1)} %get-tuple-element.16.band_ref, ...), custom_call_target="tpu_custom_call" | custom-call | flops 6442450944 | bytes 12582912 | tf_op jit(solution)/shard_map/pallas_call | solution.py:205
  125.2 0.4 collective-permute-start.10
  125.6 29.7 %shard_map.119 = (f32[1,16,32,1024]{3,2,1,0:T(8,128)}, bf16[1,16,32,1024]{3,2,1,0:T(8,128)(2,1)}) custom-call(s32[128]{0:T(128)} %reshape.211.strip_ref, bf16[4,128,4224]{2,1,0:T(8,128)(2,1)} %pad.32.x_ref.halo_ref, bf16[4,128,4224]{2,1,0:T(8,128)(2,1)} %pad.32.x_ref.halo_ref, bf16[32,256,256]{2,1,0:T(8,128)(2,1)} %get-tuple-element.16.band_ref, ...), custom_call_target="tpu_custom_call" | custom-call | flops 6442450944 | bytes 12582912 | tf_op jit(solution)/shard_map/pallas_call | solution.py:205
  155.4 0.3 bitcast_add_fusion.3
  155.8 3.0 %collective-permute-start.1 = (bf16[8,32,1024]{2,1,0:T(8,128)(2,1)S(1)}, bf16[8,32,1024]{2,1,0:T(8,128)(2,1)S(1)}, u32[]{:S(2)}, u32[]{:S(2)}) collective-permute-start(bf16[8,32,1024]{2,1,0:T(8,128)(2,1)S(1)} %slice.261), channel_id=1, source_target_pairs={{0,2},{2,0},{4,6},{6,4},{8,10},{10,8},{12,14},{14,12},{16,18},{18,... | collective-permute-start | bytes 1572872 | tf_op jit(solution)/shard_map/ppermute | solution.py:140
  158.8 0.5 bitcast_add_fusion.2
  159.3 1.6 collective-permute-start.6
  160.9 0.5 bitcast_add_fusion.1
  161.5 1.2 collective-permute-start.11
  162.7 0.4 bitcast_add_fusion
  163.2 1.0 collective-permute-start.16
  164.2 7.3 %collective-permute-done.1 = bf16[8,32,1024]{2,1,0:T(8,128)(2,1)S(1)} collective-permute-done((bf16[8,32,1024]{2,1,0:T(8,128)(2,1)S(1)}, bf16[8,32,1024]{2,1,0:T(8,128)(2,1)S(1)}, u32[]{:S(2)}, u32[]{:S(2)}) %collective-permute-start.1) | collective-permute-done | bytes 524320 | tf_op jit(solution)/shard_map/ppermute | solution.py:140
  171.5 0.2 slice_add_fusion.3
  171.8 2.2 %collective-permute-start.2 = (bf16[4,32,1024]{2,1,0:T(8,128)(2,1)S(1)}, bf16[4,32,1024]{2,1,0:T(8,128)(2,1)S(1)}, u32[]{:S(2)}, u32[]{:S(2)}) collective-permute-start(bf16[4,32,1024]{2,1,0:T(8,128)(2,1)S(1)} %slice.265), channel_id=1, source_target_pairs={{0,4},{2,6},{4,0},{6,2},{8,12},{10,14},{12,8},{14,10},{16,20},{18,... | collective-permute-start | bytes 786440 | tf_op jit(solution)/shard_map/ppermute | solution.py:140
  173.9 0.3 collective-permute-done.6
  174.2 0.2 slice_add_fusion.2
  174.5 1.2 collective-permute-start.7
  175.7 7.1 %collective-permute-done.11 = bf16[8,32,1024]{2,1,0:T(8,128)(2,1)S(1)} collective-permute-done((bf16[8,32,1024]{2,1,0:T(8,128)(2,1)S(1)}, bf16[8,32,1024]{2,1,0:T(8,128)(2,1)S(1)}, u32[]{:S(2)}, u32[]{:S(2)}) %collective-permute-start.11) | collective-permute-done | bytes 524320 | tf_op jit(solution)/shard_map/ppermute | solution.py:140
  182.8 0.1 slice_add_fusion.1
  182.9 2.2 %collective-permute-start.12 = (bf16[4,32,1024]{2,1,0:T(8,128)(2,1)S(1)}, bf16[4,32,1024]{2,1,0:T(8,128)(2,1)S(1)}, u32[]{:S(2)}, u32[]{:S(2)}) collective-permute-start(bf16[4,32,1024]{2,1,0:T(8,128)(2,1)S(1)} %slice.263), channel_id=1, source_target_pairs={{0,4},{2,6},{4,0},{6,2},{8,12},{10,14},{12,8},{14,10},{16,20},{18,... | collective-permute-start | bytes 786440 | tf_op jit(solution)/shard_map/ppermute | solution.py:140
  185.1 0.4 collective-permute-done.16
  185.5 0.2 slice_add_fusion
  185.7 1.2 collective-permute-start.17
  186.9 4.2 %collective-permute-done.2 = bf16[4,32,1024]{2,1,0:T(8,128)(2,1)S(1)} collective-permute-done((bf16[4,32,1024]{2,1,0:T(8,128)(2,1)S(1)}, bf16[4,32,1024]{2,1,0:T(8,128)(2,1)S(1)}, u32[]{:S(2)}, u32[]{:S(2)}) %collective-permute-start.2) | collective-permute-done | bytes 262176 | tf_op jit(solution)/shard_map/ppermute | solution.py:140
  191.2 1.7 collective-permute-start.3
  192.9 0.5 collective-permute-start.8
  193.4 2.0 collective-permute-done.12
  195.6 1.7 collective-permute-start.13
  197.3 0.5 collective-permute-start.18
  197.9 2.6 %collective-permute-start.4 = (bf16[1,32,1024]{2,1,0:T(8,128)(2,1)S(1)}, bf16[1,32,1024]{2,1,0:T(8,128)(2,1)S(1)}, u32[]{:S(2)}, u32[]{:S(2)}) collective-permute-start(bf16[1,32,1024]{2,1,0:T(8,128)(2,1)S(1)} %slice.273), channel_id=1, source_target_pairs={{0,16},{2,18},{4,20},{6,22},{8,24},{10,26},{12,28},{14,30},{16,0},... | collective-permute-start | bytes 196616 | tf_op jit(solution)/shard_map/ppermute | solution.py:140
  200.6 1.1 collective-permute-start.9
  201.7 3.2 %collective-permute-done.13 = bf16[2,32,1024]{2,1,0:T(8,128)(2,1)S(1)} collective-permute-done((bf16[2,32,1024]{2,1,0:T(8,128)(2,1)S(1)}, bf16[2,32,1024]{2,1,0:T(8,128)(2,1)S(1)}, u32[]{:S(2)}, u32[]{:S(2)}) %collective-permute-start.13) | collective-permute-done | bytes 131104 | tf_op jit(solution)/shard_map/ppermute | solution.py:140
  204.9 0.8 collective-permute-start.14
  205.8 1.3 collective-permute-done.18
  207.2 0.9 collective-permute-start.19
  208.1 3.9 %collective-permute-done.14 = bf16[1,32,1024]{2,1,0:T(8,128)(2,1)S(1)} collective-permute-done((bf16[1,32,1024]{2,1,0:T(8,128)(2,1)S(1)}, bf16[1,32,1024]{2,1,0:T(8,128)(2,1)S(1)}, u32[]{:S(2)}, u32[]{:S(2)}) %collective-permute-start.14) | collective-permute-done | bytes 65568 | tf_op jit(solution)/shard_map/ppermute | solution.py:140
  212.0 1.4 collective-permute-done.19
  213.4 0.8 pad_maximum_fusion
  (62 shorter events, 1.4 us)
Async XLA Ops:
  12.6 7.8 %copy-start.4 = (f32[192,248,1]{1,0,2:T(8,128)S(1)}, f32[192,248,1]{1,0,2:T(8,128)}, u32[]{:S(2)}) copy-start(f32[192,248,1]{1,0,2:T(8,128)} %constant.96) | copy-start | bytes 571396
  65.7 89.7 %collective-permute-start = (bf16[16,32,1024]{2,1,0:T(8,128)(2,1)}, bf16[16,32,1024]{2,1,0:T(8,128)(2,1)S(1)}, u32[]{:S(2)}, u32[]{:S(2)}) collective-permute-start(bf16[16,32,1024]{2,1,0:T(8,128)(2,1)} %bitcast.59), channel_id=1, source_target_pairs={{0,1},{1,0},{2,3},{3,2},{4,5},{5,4},{6,7},{7,6},{8,9},{9,8},{10,11... | collective-permute-start | bytes 3145736 | tf_op jit(solution)/shard_map/ppermute | solution.py:140
  95.6 63.2 %collective-permute-start.5 = (bf16[16,32,1024]{2,1,0:T(8,128)(2,1)}, bf16[16,32,1024]{2,1,0:T(8,128)(2,1)S(1)}, u32[]{:S(2)}, u32[]{:S(2)}) collective-permute-start(bf16[16,32,1024]{2,1,0:T(8,128)(2,1)} %bitcast.58), channel_id=1, source_target_pairs={{0,1},{1,0},{2,3},{3,2},{4,5},{5,4},{6,7},{7,6},{8,9},{9,8},{10,11... | collective-permute-start | bytes 3145736 | tf_op jit(solution)/shard_map/ppermute | solution.py:140
  125.2 30.2 %copy-start.3 = (f32[1,16,32,1024]{3,2,1,0:T(8,128)S(1)}, f32[1,16,32,1024]{3,2,1,0:T(8,128)}, u32[]{:S(2)}) copy-start(f32[1,16,32,1024]{3,2,1,0:T(8,128)} %get-tuple-element.18) | copy-start | bytes 6291460
  125.2 35.8 %collective-permute-start.10 = (bf16[16,32,1024]{2,1,0:T(8,128)(2,1)}, bf16[16,32,1024]{2,1,0:T(8,128)(2,1)S(1)}, u32[]{:S(2)}, u32[]{:S(2)}) collective-permute-start(bf16[16,32,1024]{2,1,0:T(8,128)(2,1)} %bitcast.57), channel_id=1, source_target_pairs={{0,1},{1,0},{2,3},{3,2},{4,5},{5,4},{6,7},{7,6},{8,9},{9,8},{10,11... | collective-permute-start | bytes 3145736 | tf_op jit(solution)/shard_map/ppermute | solution.py:140
  155.3 7.3 %collective-permute-start.15 = (bf16[16,32,1024]{2,1,0:T(8,128)(2,1)}, bf16[16,32,1024]{2,1,0:T(8,128)(2,1)S(1)}, u32[]{:S(2)}, u32[]{:S(2)}) collective-permute-start(bf16[16,32,1024]{2,1,0:T(8,128)(2,1)} %bitcast.56), channel_id=1, source_target_pairs={{0,1},{1,0},{2,3},{3,2},{4,5},{5,4},{6,7},{7,6},{8,9},{9,8},{10,11... | collective-permute-start | bytes 3145736 | tf_op jit(solution)/shard_map/ppermute | solution.py:140
  155.4 3.4 %copy-start.2 = (f32[1,16,32,1024]{3,2,1,0:T(8,128)S(1)}, f32[1,16,32,1024]{3,2,1,0:T(8,128)}, u32[]{:S(2)}) copy-start(f32[1,16,32,1024]{3,2,1,0:T(8,128)} %get-tuple-element.20) | copy-start | bytes 6291460
  155.8 15.7 %collective-permute-start.1 = (bf16[8,32,1024]{2,1,0:T(8,128)(2,1)S(1)}, bf16[8,32,1024]{2,1,0:T(8,128)(2,1)S(1)}, u32[]{:S(2)}, u32[]{:S(2)}) collective-permute-start(bf16[8,32,1024]{2,1,0:T(8,128)(2,1)S(1)} %slice.261), channel_id=1, source_target_pairs={{0,2},{2,0},{4,6},{6,4},{8,10},{10,8},{12,14},{14,12},{16,18},{18,... | collective-permute-start | bytes 1572872 | tf_op jit(solution)/shard_map/ppermute | solution.py:140
  158.8 2.1 copy-start.1
  159.3 14.9 %collective-permute-start.6 = (bf16[8,32,1024]{2,1,0:T(8,128)(2,1)S(1)}, bf16[8,32,1024]{2,1,0:T(8,128)(2,1)S(1)}, u32[]{:S(2)}, u32[]{:S(2)}) collective-permute-start(bf16[8,32,1024]{2,1,0:T(8,128)(2,1)S(1)} %slice.260), channel_id=1, source_target_pairs={{0,4},{2,6},{4,0},{6,2},{8,12},{10,14},{12,8},{14,10},{16,20},{18,... | collective-permute-start | bytes 1572872 | tf_op jit(solution)/shard_map/ppermute | solution.py:140
  160.9 1.7 copy-start
  161.5 21.3 %collective-permute-start.11 = (bf16[8,32,1024]{2,1,0:T(8,128)(2,1)S(1)}, bf16[8,32,1024]{2,1,0:T(8,128)(2,1)S(1)}, u32[]{:S(2)}, u32[]{:S(2)}) collective-permute-start(bf16[8,32,1024]{2,1,0:T(8,128)(2,1)S(1)} %slice.259), channel_id=1, source_target_pairs={{0,2},{2,0},{4,6},{6,4},{8,10},{10,8},{12,14},{14,12},{16,18},{18,... | collective-permute-start | bytes 1572872 | tf_op jit(solution)/shard_map/ppermute | solution.py:140
  163.2 22.3 %collective-permute-start.16 = (bf16[8,32,1024]{2,1,0:T(8,128)(2,1)S(1)}, bf16[8,32,1024]{2,1,0:T(8,128)(2,1)S(1)}, u32[]{:S(2)}, u32[]{:S(2)}) collective-permute-start(bf16[8,32,1024]{2,1,0:T(8,128)(2,1)S(1)} %slice.258), channel_id=1, source_target_pairs={{0,4},{2,6},{4,0},{6,2},{8,12},{10,14},{12,8},{14,10},{16,20},{18,... | collective-permute-start | bytes 1572872 | tf_op jit(solution)/shard_map/ppermute | solution.py:140
  171.8 19.3 %collective-permute-start.2 = (bf16[4,32,1024]{2,1,0:T(8,128)(2,1)S(1)}, bf16[4,32,1024]{2,1,0:T(8,128)(2,1)S(1)}, u32[]{:S(2)}, u32[]{:S(2)}) collective-permute-start(bf16[4,32,1024]{2,1,0:T(8,128)(2,1)S(1)} %slice.265), channel_id=1, source_target_pairs={{0,4},{2,6},{4,0},{6,2},{8,12},{10,14},{12,8},{14,10},{16,20},{18,... | collective-permute-start | bytes 786440 | tf_op jit(solution)/shard_map/ppermute | solution.py:140
  174.5 18.4 %collective-permute-start.7 = (bf16[4,32,1024]{2,1,0:T(8,128)(2,1)S(1)}, bf16[4,32,1024]{2,1,0:T(8,128)(2,1)S(1)}, u32[]{:S(2)}, u32[]{:S(2)}) collective-permute-start(bf16[4,32,1024]{2,1,0:T(8,128)(2,1)S(1)} %slice.264), channel_id=1, source_target_pairs={{0,2},{2,0},{4,6},{6,4},{8,10},{10,8},{12,14},{14,12},{16,18},{18,... | collective-permute-start | bytes 786440 | tf_op jit(solution)/shard_map/ppermute | solution.py:140
  182.9 12.5 %collective-permute-start.12 = (bf16[4,32,1024]{2,1,0:T(8,128)(2,1)S(1)}, bf16[4,32,1024]{2,1,0:T(8,128)(2,1)S(1)}, u32[]{:S(2)}, u32[]{:S(2)}) collective-permute-start(bf16[4,32,1024]{2,1,0:T(8,128)(2,1)S(1)} %slice.263), channel_id=1, source_target_pairs={{0,4},{2,6},{4,0},{6,2},{8,12},{10,14},{12,8},{14,10},{16,20},{18,... | collective-permute-start | bytes 786440 | tf_op jit(solution)/shard_map/ppermute | solution.py:140
  185.7 11.5 %collective-permute-start.17 = (bf16[4,32,1024]{2,1,0:T(8,128)(2,1)S(1)}, bf16[4,32,1024]{2,1,0:T(8,128)(2,1)S(1)}, u32[]{:S(2)}, u32[]{:S(2)}) collective-permute-start(bf16[4,32,1024]{2,1,0:T(8,128)(2,1)S(1)} %slice.262), channel_id=1, source_target_pairs={{0,2},{2,0},{4,6},{6,4},{8,10},{10,8},{12,14},{14,12},{16,18},{18,... | collective-permute-start | bytes 786440 | tf_op jit(solution)/shard_map/ppermute | solution.py:140
  191.2 6.6 %collective-permute-start.3 = (bf16[2,32,1024]{2,1,0:T(8,128)(2,1)S(1)}, bf16[2,32,1024]{2,1,0:T(8,128)(2,1)S(1)}, u32[]{:S(2)}, u32[]{:S(2)}) collective-permute-start(bf16[2,32,1024]{2,1,0:T(8,128)(2,1)S(1)} %slice.269), channel_id=1, source_target_pairs={{0,8},{2,10},{4,12},{6,14},{8,0},{10,2},{12,4},{14,6},{16,24},{18,... | collective-permute-start | bytes 393224 | tf_op jit(solution)/shard_map/ppermute | solution.py:140
  192.9 7.6 %collective-permute-start.8 = (bf16[2,32,1024]{2,1,0:T(8,128)(2,1)S(1)}, bf16[2,32,1024]{2,1,0:T(8,128)(2,1)S(1)}, u32[]{:S(2)}, u32[]{:S(2)}) collective-permute-start(bf16[2,32,1024]{2,1,0:T(8,128)(2,1)S(1)} %slice.268), channel_id=1, source_target_pairs={{0,8},{2,10},{4,12},{6,14},{8,0},{10,2},{12,4},{14,6},{16,24},{18,... | collective-permute-start | bytes 393224 | tf_op jit(solution)/shard_map/ppermute | solution.py:140
  195.6 9.3 %collective-permute-start.13 = (bf16[2,32,1024]{2,1,0:T(8,128)(2,1)S(1)}, bf16[2,32,1024]{2,1,0:T(8,128)(2,1)S(1)}, u32[]{:S(2)}, u32[]{:S(2)}) collective-permute-start(bf16[2,32,1024]{2,1,0:T(8,128)(2,1)S(1)} %slice.267), channel_id=1, source_target_pairs={{0,8},{2,10},{4,12},{6,14},{8,0},{10,2},{12,4},{14,6},{16,24},{18,... | collective-permute-start | bytes 393224 | tf_op jit(solution)/shard_map/ppermute | solution.py:140
  197.3 9.8 %collective-permute-start.18 = (bf16[2,32,1024]{2,1,0:T(8,128)(2,1)S(1)}, bf16[2,32,1024]{2,1,0:T(8,128)(2,1)S(1)}, u32[]{:S(2)}, u32[]{:S(2)}) collective-permute-start(bf16[2,32,1024]{2,1,0:T(8,128)(2,1)S(1)} %slice.266), channel_id=1, source_target_pairs={{0,8},{2,10},{4,12},{6,14},{8,0},{10,2},{12,4},{14,6},{16,24},{18,... | collective-permute-start | bytes 393224 | tf_op jit(solution)/shard_map/ppermute | solution.py:140
  197.9 10.2 %collective-permute-start.4 = (bf16[1,32,1024]{2,1,0:T(8,128)(2,1)S(1)}, bf16[1,32,1024]{2,1,0:T(8,128)(2,1)S(1)}, u32[]{:S(2)}, u32[]{:S(2)}) collective-permute-start(bf16[1,32,1024]{2,1,0:T(8,128)(2,1)S(1)} %slice.273), channel_id=1, source_target_pairs={{0,16},{2,18},{4,20},{6,22},{8,24},{10,26},{12,28},{14,30},{16,0},... | collective-permute-start | bytes 196616 | tf_op jit(solution)/shard_map/ppermute | solution.py:140
  200.6 7.5 %collective-permute-start.9 = (bf16[1,32,1024]{2,1,0:T(8,128)(2,1)S(1)}, bf16[1,32,1024]{2,1,0:T(8,128)(2,1)S(1)}, u32[]{:S(2)}, u32[]{:S(2)}) collective-permute-start(bf16[1,32,1024]{2,1,0:T(8,128)(2,1)S(1)} %slice.272), channel_id=1, source_target_pairs={{0,16},{2,18},{4,20},{6,22},{8,24},{10,26},{12,28},{14,30},{16,0},... | collective-permute-start | bytes 196616 | tf_op jit(solution)/shard_map/ppermute | solution.py:140
  204.9 7.0 %collective-permute-start.14 = (bf16[1,32,1024]{2,1,0:T(8,128)(2,1)S(1)}, bf16[1,32,1024]{2,1,0:T(8,128)(2,1)S(1)}, u32[]{:S(2)}, u32[]{:S(2)}) collective-permute-start(bf16[1,32,1024]{2,1,0:T(8,128)(2,1)S(1)} %slice.271), channel_id=1, source_target_pairs={{0,16},{2,18},{4,20},{6,22},{8,24},{10,26},{12,28},{14,30},{16,0},... | collective-permute-start | bytes 196616 | tf_op jit(solution)/shard_map/ppermute | solution.py:140
  207.2 6.2 %collective-permute-start.19 = (bf16[1,32,1024]{2,1,0:T(8,128)(2,1)S(1)}, bf16[1,32,1024]{2,1,0:T(8,128)(2,1)S(1)}, u32[]{:S(2)}, u32[]{:S(2)}) collective-permute-start(bf16[1,32,1024]{2,1,0:T(8,128)(2,1)S(1)} %slice.270), channel_id=1, source_target_pairs={{0,16},{2,18},{4,20},{6,22},{8,24},{10,26},{12,28},{14,30},{16,0},... | collective-permute-start | bytes 196616 | tf_op jit(solution)/shard_map/ppermute | solution.py:140
where the time goes:
time: 215 us; the launch traced here: 214 us
  Pallas kernels  126 us (59%)
  waiting for transfers between devices  31.1 us (14%)
  starting transfers between devices  24.3 us (11%)
  local copies, waits for them, and re-layouts  17 us (8%)
  other arithmetic  14.3 us (7%)
    pallas_call x4, Pallas kernels, shards(): pl.pallas_call(functools.partial(main_kernel, tuple(order), streams), gri...  118 us
    ppermute x20, waiting for transfers between devices, swap(): return lax.ppermute(x, axis, [(i, i ^ bit) for i in range(n)])  31.1 us
    ppermute x20, starting transfers between devices, swap(): return lax.ppermute(x, axis, [(i, i ^ bit) for i in range(n)])  24.3 us
    pallas_call x1, Pallas kernels, shards(): pl.pallas_call(functools.partial(prep_kernel, streams), out_shape=(jax.Sh...  7.56 us
    pad x1, local copies, waits for them, and re-layouts, shards(): x = jnp.pad(x, ((0, 0), (0, 0), (32, 96)))  6.91 us
    mul x1, local copies, waits for them, and re-layouts, row_table(): mix.transpose(0, 2, 1)[:, :, None, :, None] * ymat[:, None, :, None, :]  6.21 us
  transfers between devices with their start and end apart: 20, of which 10 were waited for; matrix products, arithmetic and copies ran while one was open for 2% of the time, Pallas kernels for 41%

commit v1 on v0

v1 whole, which is shorter than its diff:
```python
import functools

import jax
import jax.numpy as jnp
import numpy as np
from jax import lax
from jax.experimental import pallas as pl
from jax.experimental.pallas import tpu as pltpu
from jax.sharding import PartitionSpec as P

SLAB_ROWS = 64
ROWS = 8
TAPS_OUT = 36
CHUNKS = 4
EMPTY = 128
VMEM_LIMIT = 42 * 1024 * 1024
HI = lax.Precision.HIGHEST


def lanczos_taps(fraction):
    distance = jnp.arange(6, dtype=jnp.int32).astype(jnp.float32) - 2.0 - fraction[..., None]
    values = jnp.sinc(distance) * jnp.sinc(distance / 3.0)
    return values / jnp.sum(values, axis=-1, keepdims=True)


def column_rows(basis_x, warp_x):
    summed = 0.0
    for q in range(6):
        part = basis_x[None, :, :] * warp_x[:, q, None, None]
        summed = summed + jnp.pad(part, ((0, 0), (0, 0), (q, 5 - q)))
    hx = summed.astype(jnp.bfloat16).astype(jnp.float32)
    return jnp.pad(hx[:, :, ::-1], ((0, 0), (0, 0), (206, 14)))


def row_table(weight, coeffs, basis_y, warp_y):
    bases, taps = basis_y.shape
    mix = basis_y[None] * (weight[:, None] * coeffs)[:, :, None]
    mix = mix.astype(jnp.bfloat16).astype(jnp.float32)
    i = np.arange(ROWS)
    tap = i[None, :] - i[:, None] + 2
    pick = (tap[:, :, None] == np.arange(6)).astype(np.float32)
    ymat = jnp.sum(pick[None] * warp_y[:, None, None, :], axis=3)
    ymat = ymat.astype(jnp.bfloat16).astype(jnp.float32)
    rows = jnp.repeat(mix[:, :, ::-1].transpose(0, 2, 1), ROWS, axis=2)
    lanes = jnp.tile(ymat, (1, 1, bases))
    table = 0.0
    for k in range(ROWS):
        placed = jnp.pad(rows, ((0, 0), (41 + k, 192 - taps - 41 - k), (0, 0)))
        table = table + placed * lanes[:, k : k + 1]
    return table


def prep_kernel(streams, starts_ref, me_ref, v_ref, k2_ref, band_ref, w_ref):
    pairs = v_ref.shape[0] // 2
    patches = w_ref.shape[0]
    steps = k2_ref.shape[0]
    part = SLAB_ROWS // streams

    def one_band(g, c):
        for side in range(2):
            row = v_ref[pl.ds(g * 2 + side, 1), :]
            wide = jnp.broadcast_to(row, (256, 256))
            rolled = pltpu.roll(wide, 0, 1, stride=1, stride_axis=0)
            band_ref[g, :, side * 128 : (side + 1) * 128] = rolled[:, :128].astype(jnp.bfloat16)
        return c

    lax.fori_loop(0, pairs, one_band, 0)
    me = me_ref[0]

    def one_patch(q, c):
        for t in range(steps):
            for slot in range(2):
                base = starts_ref[(q * steps + t) * 2 + slot]
                rows = [
                    k2_ref[t, pl.ds(base + part * jnp.bitwise_xor(me, s), part), :]
                    for s in range(streams)
                ]
                block = jnp.concatenate(rows, axis=0).astype(jnp.bfloat16)
                w_ref[q, :, (t * 2 + slot) * 128 : (t * 2 + slot + 1) * 128] = block
        return c

    lax.fori_loop(0, patches, one_patch, 0)


def field_sizes(bits):
    sizes = [2] * (bits // 2)
    return sizes + [1] * (bits % 2)


def main_kernel(first_block, blocks, patch_bits, streams, strip_ref, x_ref, band_ref, w_ref, keep_ref, send_ref, f_ref):
    steps = x_ref.shape[0]
    strips = x_ref.shape[1] // ROWS
    tiles = x_ref.shape[2] // 128
    patches = w_ref.shape[0]
    part = SLAB_ROWS // streams
    width = blocks * 128

    def one_step(t, c):
        pieces = []
        for n in range(first_block, first_block + blocks):
            if 0 <= n and n + 2 <= tiles:
                pieces.append(x_ref[t, :, n * 128 : n * 128 + 256])
            else:
                blank = jnp.zeros((strips * ROWS, 128), jnp.bfloat16)
                sides = [x_ref[t, :, m * 128 : (m + 1) * 128] if 0 <= m < tiles else blank for m in (n, n + 1)]
                pieces.append(jnp.concatenate(sides, axis=1))
        lhs = jnp.concatenate(pieces, axis=0)
        for g in range(8):
            res = jnp.dot(lhs, band_ref[t * 8 + g], preferred_element_type=jnp.float32)
            res = res.reshape(blocks, strips, ROWS, 256)
            for n in range(blocks):
                two = jnp.concatenate([res[n, :, :, :128], res[n, :, :, 128:]], axis=1)
                f_ref[pl.ds(t * strips, strips), g, :, n * 128 : (n + 1) * 128] = two.astype(jnp.bfloat16)
        return c

    lax.fori_loop(0, steps, one_step, 0)

    def one_patch(q):
        rhs = jnp.concatenate(
            [f_ref[strip_ref[q * steps * 2 + k]].reshape(128, width) for k in range(2 * steps)], axis=0
        )
        acc = jnp.dot(w_ref[q], rhs, preferred_element_type=jnp.float32)
        pos, low, left = 0, 0, patches
        for size in field_sizes(patch_bits):
            left = left >> size
            pos = pos + (lax.shift_right_logical(q, low) & ((1 << size) - 1)) * left
            low += size
        keep_ref[pos] = acc[:part]
        for s in range(1, streams):
            send_ref[s - 1, pos] = acc[s * part : (s + 1) * part].astype(jnp.bfloat16)

    def four(i, c):
        for k in range(4):
            one_patch(i * 4 + k)
        return c

    lax.fori_loop(0, patches // 4, four, 0)


def swap(x, axis, mask):
    n = lax.axis_size(axis)
    return lax.ppermute(x, axis, [(i, i ^ mask) for i in range(n)])


def add_all(keep, arrived):
    for one in arrived:
        keep = keep + one.astype(jnp.float32)
    return keep


def shards(
    exposures, owners, offsets, visit_shift, visit_weight, psf_class, coef_table, basis_x, basis_y
):
    patches = lax.axis_size("patch")
    streams = lax.axis_size("stream")
    my_patch = lax.axis_index("patch")
    my_stream = lax.axis_index("stream")
    steps, strips, width = exposures.shape[0], exposures.shape[2], exposures.shape[4]
    part = SLAB_ROWS // streams
    patch_bits = patches.bit_length() - 1

    x = exposures.reshape(steps, strips * ROWS, width)

    warp = lanczos_taps(visit_shift[:, 0])
    vrows = column_rows(basis_x, warp[:, 0]).reshape(-1, 256)
    hits = (psf_class[:, 0, None] == jnp.arange(coef_table.shape[0], dtype=jnp.int32)).astype(jnp.float32)
    coeffs = jnp.sum(hits[:, :, None] * coef_table[None], axis=1)
    k2 = row_table(visit_weight[:, 0], coeffs, basis_y, warp[:, 1])

    wanted = jnp.bitwise_xor(jnp.arange(patches, dtype=jnp.int32), my_patch)
    own, off = owners[:, 0], offsets[:, 0]
    match = own[None] == wanted[:, None, None, None]
    named = jnp.any(match, axis=3)
    at = jnp.sum(jnp.where(match, off[None], 0), axis=3)
    ids = jnp.arange(strips, dtype=jnp.int32)
    first = jnp.min(jnp.where(named, ids, strips), axis=2)
    last = jnp.max(jnp.where(named, ids, -1), axis=2)
    one = named & (ids == first[..., None])
    two = named & (ids == last[..., None]) & (last > first)[..., None]
    start = jnp.stack(
        [jnp.sum(jnp.where(m, 56 - at - EMPTY, 0), axis=2) + EMPTY for m in (one, two)], axis=2
    )
    base = jnp.arange(steps, dtype=jnp.int32)[None] * strips
    strip = jnp.stack([base + jnp.clip(first, 0, strips - 1), base + jnp.clip(last, 0, strips - 1)], axis=2)
    start, strip = start.reshape(-1), strip.reshape(-1)

    smem = pl.BlockSpec(memory_space=pltpu.SMEM)
    vmem = pl.BlockSpec(memory_space=pltpu.VMEM)
    params = pltpu.CompilerParams(vmem_limit_bytes=VMEM_LIMIT)
    band, w = pl.pallas_call(
        functools.partial(prep_kernel, streams),
        out_shape=(
            jax.ShapeDtypeStruct((steps * 8, 256, 256), jnp.bfloat16),
            jax.ShapeDtypeStruct((patches, SLAB_ROWS, steps * 256), jnp.bfloat16),
        ),
        in_specs=[smem, smem, vmem, vmem],
        out_specs=(vmem, vmem),
        compiler_params=params,
    )(start, my_stream.reshape(1).astype(jnp.int32), vrows, k2)

    total_blocks = width // 128 + 1
    sizes = [total_blocks // CHUNKS + (c < total_blocks % CHUNKS) for c in range(CHUNKS)]
    fields = field_sizes(patch_bits)

    def hop(total, k):
        low = sum(fields[:k])
        parts = total.reshape(1 << fields[k], -1, part, total.shape[-1])
        sends = [parts[g].astype(jnp.bfloat16) for g in range(1, 1 << fields[k])]
        return add_all(parts[0], [swap(v, "patch", (g + 1) << low) for g, v in enumerate(sends)])

    sums = []
    begin = -1
    for c, blocks in enumerate(sizes):
        wide = blocks * 128
        table = strip
        if c >= 2:
            table, *tied = lax.optimization_barrier((strip, *sums[max(0, c - 1 - len(fields)) : c - 1]))
            for k, total in enumerate(reversed(tied)):
                sums[c - 2 - k] = hop(total, k)
        keep, send = pl.pallas_call(
            functools.partial(main_kernel, begin, blocks, patch_bits, streams),
            in_specs=[smem, vmem, vmem, vmem],
            out_specs=(vmem, vmem),
            out_shape=(
                jax.ShapeDtypeStruct((patches, part, wide), jnp.float32),
                jax.ShapeDtypeStruct((streams - 1, patches, part, wide), jnp.bfloat16),
            ),
            scratch_shapes=[pltpu.VMEM((steps * strips, 8, 16, wide), jnp.bfloat16)],
            compiler_params=params,
            cost_estimate=pl.CostEstimate(flops=12 << 30, bytes_accessed=12 << 20, transcendentals=0),
        )(table, x, band, w)
        begin += blocks
        sums.append(add_all(keep, [swap(send[s - 1], "stream", s) for s in range(1, streams)]))
    for c in range(CHUNKS):
        for k in range(min(len(fields), max(0, CHUNKS - 2 - c + 0)), len(fields)):
            sums[c] = hop(sums[c], k)
    out = jnp.concatenate([total[0] for total in sums], axis=1)
    return out[:, 96 : 96 + width]


def solution(mesh):
    placed = (
        P(None, "stream", "patch", None, None),
        P(None, "stream", "patch", None),
        P(None, "stream", "patch", None),
        P(None, "stream", None),
        P(None, "stream"),
        P(None, "stream"),
        P(),
        P(),
        P(),
    )
    return jax.shard_map(
        shards, mesh=mesh, in_specs=placed, out_specs=P(("patch", "stream"), None), check_vma=False
    )
```

time: 215 us -> 144 us (0.67)
  Pallas kernels: 126 us -> 63.2 us
  local copies, waits for them, and re-layouts: 17 us -> 5.76 us
  starting transfers between devices: 24.3 us -> 31.3 us
  other arithmetic: 14.3 us -> 11.6 us
    pallas_call x4, Pallas kernels: 118 us -> 58.8 us  [shards(): pl.pallas_call(functools.partial(main_kernel, begin, blocks, patch_bits,...]
    ppermute x20 -> x28, starting transfers between devices: 24.3 us -> 31.3 us  [swap(): return lax.ppermute(x, axis, [(i, i ^ mask) for i in range(n)])]
    mul x2 -> x0, local copies, waits for them, and re-layouts: 7 us -> none  [the longest x1 6.21 us: row_table(): mix.transpose(0, 2, 1)[:, :, None, :, None] * ymat[:, None, :, None, :]]
    pad x1 -> x0, local copies, waits for them, and re-layouts: 6.91 us -> none  [shards(): x = jnp.pad(x, ((0, 0), (0, 0), (32, 96)))]
    unnamed x10 -> x4, local copies, waits for them, and re-layouts: 0.02 us -> 4.14 us
    mul x1 -> x0, other arithmetic: 3.73 us -> none  [row_table(): mix.transpose(0, 2, 1)[:, :, None, :, None] * ymat[:, None, :, None, :]]
    pallas_call x1, Pallas kernels: 7.56 us -> 4.4 us  [shards(): pl.pallas_call(functools.partial(prep_kernel, streams), out_shape=(jax.Sh...]
    ppermute x20 -> x28, waiting for transfers between devices: 31.1 us -> 31.4 us  [swap(): return lax.ppermute(x, axis, [(i, i ^ mask) for i in range(n)])]
  transfers between devices with their start and end apart: 20 -> 28, of which waited for: 10 -> 14; matrix products, arithmetic and copies ran while one was open for 2% -> 2% of each run, Pallas kernels for 41% -> 31%
where the time goes in v1:
time: 144 us
  Pallas kernels  63.2 us (44%)
  waiting for transfers between devices  31.4 us (22%)
  starting transfers between devices  31.3 us (22%)
  other arithmetic  11.6 us (8%)
  local copies, waits for them, and re-layouts  5.76 us (4%)
    pallas_call x4, Pallas kernels, shards(): pl.pallas_call(functools.partial(main_kernel, begin, blocks, patch_bits,...  58.8 us
    ppermute x28, waiting for transfers between devices, swap(): return lax.ppermute(x, axis, [(i, i ^ mask) for i in range(n)])  31.4 us
    ppermute x28, starting transfers between devices, swap(): return lax.ppermute(x, axis, [(i, i ^ mask) for i in range(n)])  31.3 us
    pallas_call x1, Pallas kernels, shards(): pl.pallas_call(functools.partial(prep_kernel, streams), out_shape=(jax.Sh...  4.4 us
    unnamed x4, local copies, waits for them, and re-layouts  4.14 us
  transfers between devices with their start and end apart: 28, of which 14 were waited for; matrix products, arithmetic and copies ran while one was open for 2% of the time, Pallas kernels for 31%

profile of v1, /device:TPU:0, one launch (start us, length us, event | category | flops | bytes accessed | tf_op | source)
XLA Modules:
  0.0 143.7 jit_solution(11633358023233155490)
XLA Ops:
  0.0 0.7 fusion.57
  0.7 0.9 fusion.54
  1.6 0.3 slice_reduce_fusion.5
  1.9 0.8 compare_reduce_fusion
  2.6 0.2 select_reduce_fusion.3
  3.2 0.8 multiply_reduce_fusion.1
  4.0 0.7 broadcast_multiply_fusion.6
  4.7 0.8 fusion.18
  5.5 0.8 fusion.13
  6.3 0.3 select_reduce_fusion.1
  6.9 0.8 broadcast_multiply_fusion.5
  8.1 0.8 multiply_reduce_fusion
  9.3 4.4 %shard_map.106 = (bf16[32,256,256]{2,1,0:T(8,128)(2,1)S(1)}, bf16[16,64,1024]{2,1,0:T(8,128)(2,1)S(1)}) custom-call(s32[128]{0:T(128)S(1)} %reshape.282.starts_ref, s32[1]{0:T(128)} %bitcast.7.me_ref, f32[64,256]{1,0:T(8,128)S(1)} %bitcast.45, f32[4,192,128]{2,1,0:T(8,128)S(1)} %multiply_add_fusion.k2_ref), custom_call_target="tpu_custom_call" | custom-call | tf_op jit(solution)/shard_map/pallas_call | solution.py:190
  13.7 1.9 %copy-done.1 = bf16[32,256,256]{2,1,0:T(8,128)(2,1)} copy-done((bf16[32,256,256]{2,1,0:T(8,128)(2,1)}, bf16[32,256,256]{2,1,0:T(8,128)(2,1)S(1)}, u32[]{:S(2)}) %copy-start.1) | copy-done | bytes 4194328
  15.7 2.2 %copy-done = bf16[4,1,16,8,4096]{4,3,2,1,0:T(8,128)(2,1)S(1)} copy-done((bf16[4,1,16,8,4096]{4,3,2,1,0:T(8,128)(2,1)S(1)}, bf16[4,1,16,8,4096]{4,3,2,1,0:T(8,128)(2,1)}, u32[]{:S(2)}) %copy-start) | copy-done | bytes 4194328
  17.8 14.6 %shard_map.108 = (f32[16,32,1024]{2,1,0:T(8,128)S(1)}, bf16[1,16,32,1024]{3,2,1,0:T(8,128)(2,1)S(1)}) custom-call(s32[128]{0:T(128)S(1)} %reshape.280.strip_ref, bf16[4,128,4096]{2,1,0:T(8,128)(2,1)S(1)} %bitcast.46, bf16[32,256,256]{2,1,0:T(8,128)(2,1)} %copy-done.1, bf16[16,64,1024]{2,1,0:T(8,128)(2,1)S(1)} %get-tuple-element.22.w_ref), custom_call_target="tpu_custom_call" | custom-call | flops 12884901888 | bytes 12582912 | tf_op jit(solution)/shard_map/pallas_call | solution.py:220
  32.5 0.5 collective-permute-start.4
  33.0 14.8 %shard_map.107 = (f32[16,32,1152]{2,1,0:T(8,128)S(1)}, bf16[1,16,32,1152]{3,2,1,0:T(8,128)(2,1)S(1)}) custom-call(s32[128]{0:T(128)S(1)} %reshape.280.strip_ref, bf16[4,128,4096]{2,1,0:T(8,128)(2,1)S(1)} %bitcast.47, bf16[32,256,256]{2,1,0:T(8,128)(2,1)} %copy-done.1, bf16[16,64,1024]{2,1,0:T(8,128)(2,1)S(1)} %get-tuple-element.22.w_ref), custom_call_target="tpu_custom_call" | custom-call | flops 12884901888 | bytes 12582912 | tf_op jit(solution)/shard_map/pallas_call | solution.py:220
  47.9 0.5 convert_add_fusion.3
  48.4 2.3 %collective-permute-done = bf16[16,32,1152]{2,1,0:T(8,128)(2,1)S(1)} collective-permute-done((bf16[16,32,1152]{2,1,0:T(8,128)(2,1)S(1)}, bf16[16,32,1152]{2,1,0:T(8,128)(2,1)S(1)}, u32[]{:S(2)}, u32[]{:S(2)}) %collective-permute-start) | collective-permute-done | bytes 1179680 | tf_op jit(solution)/shard_map/ppermute | solution.py:142
  50.7 0.3 convert_add_fusion
  51.3 2.7 %collective-permute-start.1 = (bf16[4,32,1152]{2,1,0:T(8,128)(2,1)S(1)}, bf16[4,32,1152]{2,1,0:T(8,128)(2,1)S(1)}, u32[]{:S(2)}, u32[]{:S(2)}) collective-permute-start(bf16[4,32,1152]{2,1,0:T(8,128)(2,1)S(1)} %get-tuple-element.56), channel_id=1, source_target_pairs={{0,2},{2,0},{4,6},{6,4},{8,10},{10,8},{12,14},{14,12},{16,18},{18,... | collective-permute-start | bytes 884744 | tf_op jit(solution)/shard_map/ppermute | solution.py:142
  54.0 1.5 %collective-permute-start.3 = (bf16[4,32,1152]{2,1,0:T(8,128)(2,1)S(1)}, bf16[4,32,1152]{2,1,0:T(8,128)(2,1)S(1)}, u32[]{:S(2)}, u32[]{:S(2)}) collective-permute-start(bf16[4,32,1152]{2,1,0:T(8,128)(2,1)S(1)} %get-tuple-element.57), channel_id=1, source_target_pairs={{0,6},{2,4},{4,2},{6,0},{8,14},{10,12},{12,10},{14,8},{16,22},{18,... | collective-permute-start | bytes 884744 | tf_op jit(solution)/shard_map/ppermute | solution.py:142
  55.5 14.6 %shard_map.109 = (f32[16,32,1024]{2,1,0:T(8,128)S(1)}, bf16[1,16,32,1024]{3,2,1,0:T(8,128)(2,1)S(1)}) custom-call(s32[128]{0:T(128)S(1)} %reshape.280.strip_ref, bf16[4,128,4096]{2,1,0:T(8,128)(2,1)S(1)} %bitcast.48, bf16[32,256,256]{2,1,0:T(8,128)(2,1)} %copy-done.1, bf16[16,64,1024]{2,1,0:T(8,128)(2,1)S(1)} %get-tuple-element.22.w_ref), custom_call_target="tpu_custom_call" | custom-call | flops 12884901888 | bytes 12582912 | tf_op jit(solution)/shard_map/pallas_call | solution.py:220
  70.2 0.3 collective-permute-done.2
  70.7 1.8 %collective-permute-start.5 = (bf16[1,32,1152]{2,1,0:T(8,128)(2,1)S(1)}, bf16[1,32,1152]{2,1,0:T(8,128)(2,1)S(1)}, u32[]{:S(2)}, u32[]{:S(2)}) collective-permute-start(bf16[1,32,1152]{2,1,0:T(8,128)(2,1)S(1)} %get-tuple-element.68), channel_id=1, source_target_pairs={{0,8},{2,10},{4,12},{6,14},{8,0},{10,2},{12,4},{14,6},{16,24},{18,... | collective-permute-start | bytes 221192 | tf_op jit(solution)/shard_map/ppermute | solution.py:142
  72.8 1.6 %collective-permute-start.8 = (bf16[4,32,1024]{2,1,0:T(8,128)(2,1)S(1)}, bf16[4,32,1024]{2,1,0:T(8,128)(2,1)S(1)}, u32[]{:S(2)}, u32[]{:S(2)}) collective-permute-start(bf16[4,32,1024]{2,1,0:T(8,128)(2,1)S(1)} %get-tuple-element.59), channel_id=1, source_target_pairs={{0,2},{2,0},{4,6},{6,4},{8,10},{10,8},{12,14},{14,12},{16,18},{18,... | collective-permute-start | bytes 786440 | tf_op jit(solution)/shard_map/ppermute | solution.py:142
  74.3 1.5 %collective-permute-start.10 = (bf16[4,32,1024]{2,1,0:T(8,128)(2,1)S(1)}, bf16[4,32,1024]{2,1,0:T(8,128)(2,1)S(1)}, u32[]{:S(2)}, u32[]{:S(2)}) collective-permute-start(bf16[4,32,1024]{2,1,0:T(8,128)(2,1)S(1)} %get-tuple-element.60), channel_id=1, source_target_pairs={{0,6},{2,4},{4,2},{6,0},{8,14},{10,12},{12,10},{14,8},{16,22},{18,... | collective-permute-start | bytes 786440 | tf_op jit(solution)/shard_map/ppermute | solution.py:142
  75.8 0.5 collective-permute-start.9
  76.3 14.8 %shard_map.110 = (f32[16,32,1024]{2,1,0:T(8,128)S(1)}, bf16[1,16,32,1024]{3,2,1,0:T(8,128)(2,1)S(1)}) custom-call(s32[128]{0:T(128)S(1)} %reshape.280.strip_ref, bf16[4,128,4096]{2,1,0:T(8,128)(2,1)S(1)} %bitcast.49, bf16[32,256,256]{2,1,0:T(8,128)(2,1)} %copy-done.1, bf16[16,64,1024]{2,1,0:T(8,128)(2,1)S(1)} %get-tuple-element.22.w_ref), custom_call_target="tpu_custom_call" | custom-call | flops 12884901888 | bytes 12582912 | tf_op jit(solution)/shard_map/pallas_call | solution.py:220
  91.1 2.5 %collective-permute-start.7 = (bf16[1,32,1152]{2,1,0:T(8,128)(2,1)S(1)}, bf16[1,32,1152]{2,1,0:T(8,128)(2,1)S(1)}, u32[]{:S(2)}, u32[]{:S(2)}) collective-permute-start(bf16[1,32,1152]{2,1,0:T(8,128)(2,1)S(1)} %get-tuple-element.69), channel_id=1, source_target_pairs={{0,24},{2,26},{4,28},{6,30},{8,16},{10,18},{12,20},{14,22},{16,8},... | collective-permute-start | bytes 221192 | tf_op jit(solution)/shard_map/ppermute | solution.py:142
  93.7 0.2 collective-permute-start.6
  93.9 0.2 fusion.70
  94.1 1.8 %collective-permute-start.11 = (bf16[1,32,1024]{2,1,0:T(8,128)(2,1)S(1)}, bf16[1,32,1024]{2,1,0:T(8,128)(2,1)S(1)}, u32[]{:S(2)}, u32[]{:S(2)}) collective-permute-start(bf16[1,32,1024]{2,1,0:T(8,128)(2,1)S(1)} %get-tuple-element.71), channel_id=1, source_target_pairs={{0,8},{2,10},{4,12},{6,14},{8,0},{10,2},{12,4},{14,6},{16,24},{18,... | collective-permute-start | bytes 196616 | tf_op jit(solution)/shard_map/ppermute | solution.py:142
  95.9 2.3 %collective-permute-done.7 = bf16[1,32,1152]{2,1,0:T(8,128)(2,1)S(1)} collective-permute-done((bf16[1,32,1152]{2,1,0:T(8,128)(2,1)S(1)}, bf16[1,32,1152]{2,1,0:T(8,128)(2,1)S(1)}, u32[]{:S(2)}, u32[]{:S(2)}) %collective-permute-start.7) | collective-permute-done | bytes 73760 | tf_op jit(solution)/shard_map/ppermute | solution.py:142
  98.1 1.7 %collective-permute-start.13 = (bf16[1,32,1024]{2,1,0:T(8,128)(2,1)S(1)}, bf16[1,32,1024]{2,1,0:T(8,128)(2,1)S(1)}, u32[]{:S(2)}, u32[]{:S(2)}) collective-permute-start(bf16[1,32,1024]{2,1,0:T(8,128)(2,1)S(1)} %get-tuple-element.72), channel_id=1, source_target_pairs={{0,24},{2,26},{4,28},{6,30},{8,16},{10,18},{12,20},{14,22},{16,8},... | collective-permute-start | bytes 196616 | tf_op jit(solution)/shard_map/ppermute | solution.py:142
  99.9 1.6 %collective-permute-done.6 = bf16[1,32,1152]{2,1,0:T(8,128)(2,1)S(1)} collective-permute-done((bf16[1,32,1152]{2,1,0:T(8,128)(2,1)S(1)}, bf16[1,32,1152]{2,1,0:T(8,128)(2,1)S(1)}, u32[]{:S(2)}, u32[]{:S(2)}) %collective-permute-start.6) | collective-permute-done | bytes 73760 | tf_op jit(solution)/shard_map/ppermute | solution.py:142
  101.6 2.7 %collective-permute-done.13 = bf16[1,32,1024]{2,1,0:T(8,128)(2,1)S(1)} collective-permute-done((bf16[1,32,1024]{2,1,0:T(8,128)(2,1)S(1)}, bf16[1,32,1024]{2,1,0:T(8,128)(2,1)S(1)}, u32[]{:S(2)}, u32[]{:S(2)}) %collective-permute-start.13) | collective-permute-done | bytes 65568 | tf_op jit(solution)/shard_map/ppermute | solution.py:142
  104.3 3.0 %collective-permute-done.12 = bf16[1,32,1024]{2,1,0:T(8,128)(2,1)S(1)} collective-permute-done((bf16[1,32,1024]{2,1,0:T(8,128)(2,1)S(1)}, bf16[1,32,1024]{2,1,0:T(8,128)(2,1)S(1)}, u32[]{:S(2)}, u32[]{:S(2)}) %collective-permute-start.12) | collective-permute-done | bytes 65568 | tf_op jit(solution)/shard_map/ppermute | solution.py:142
  107.4 0.5 fusion.73
  107.9 1.3 collective-permute-start.15
  109.2 1.5 %collective-permute-start.17 = (bf16[4,32,1024]{2,1,0:T(8,128)(2,1)S(1)}, bf16[4,32,1024]{2,1,0:T(8,128)(2,1)S(1)}, u32[]{:S(2)}, u32[]{:S(2)}) collective-permute-start(bf16[4,32,1024]{2,1,0:T(8,128)(2,1)S(1)} %get-tuple-element.63), channel_id=1, source_target_pairs={{0,6},{2,4},{4,2},{6,0},{8,14},{10,12},{12,10},{14,8},{16,22},{18,... | collective-permute-start | bytes 786440 | tf_op jit(solution)/shard_map/ppermute | solution.py:142
  110.7 0.8 collective-permute-start.16
  111.4 0.5 fusion.76
  112.0 1.3 collective-permute-start.22
  113.3 1.5 %collective-permute-start.24 = (bf16[4,32,1024]{2,1,0:T(8,128)(2,1)S(1)}, bf16[4,32,1024]{2,1,0:T(8,128)(2,1)S(1)}, u32[]{:S(2)}, u32[]{:S(2)}) collective-permute-start(bf16[4,32,1024]{2,1,0:T(8,128)(2,1)S(1)} %get-tuple-element.66), channel_id=1, source_target_pairs={{0,6},{2,4},{4,2},{6,0},{8,14},{10,12},{12,10},{14,8},{16,22},{18,... | collective-permute-start | bytes 786440 | tf_op jit(solution)/shard_map/ppermute | solution.py:142
  114.8 2.4 %collective-permute-done.15 = bf16[4,32,1024]{2,1,0:T(8,128)(2,1)S(1)} collective-permute-done((bf16[4,32,1024]{2,1,0:T(8,128)(2,1)S(1)}, bf16[4,32,1024]{2,1,0:T(8,128)(2,1)S(1)}, u32[]{:S(2)}, u32[]{:S(2)}) %collective-permute-start.15) | collective-permute-done | bytes 262176 | tf_op jit(solution)/shard_map/ppermute | solution.py:142
  117.2 1.3 collective-permute-start.23
  118.4 5.1 %collective-permute-done.17 = bf16[4,32,1024]{2,1,0:T(8,128)(2,1)S(1)} collective-permute-done((bf16[4,32,1024]{2,1,0:T(8,128)(2,1)S(1)}, bf16[4,32,1024]{2,1,0:T(8,128)(2,1)S(1)}, u32[]{:S(2)}, u32[]{:S(2)}) %collective-permute-start.17) | collective-permute-done | bytes 262176 | tf_op jit(solution)/shard_map/ppermute | solution.py:142
  123.5 2.1 %collective-permute-done.16 = bf16[4,32,1024]{2,1,0:T(8,128)(2,1)S(1)} collective-permute-done((bf16[4,32,1024]{2,1,0:T(8,128)(2,1)S(1)}, bf16[4,32,1024]{2,1,0:T(8,128)(2,1)S(1)}, u32[]{:S(2)}, u32[]{:S(2)}) %collective-permute-start.16) | collective-permute-done | bytes 262176 | tf_op jit(solution)/shard_map/ppermute | solution.py:142
  125.6 0.2 fusion.71
  125.8 0.3 collective-permute-start.18
  126.1 2.3 %collective-permute-start.20 = (bf16[1,32,1024]{2,1,0:T(8,128)(2,1)S(1)}, bf16[1,32,1024]{2,1,0:T(8,128)(2,1)S(1)}, u32[]{:S(2)}, u32[]{:S(2)}) collective-permute-start(bf16[1,32,1024]{2,1,0:T(8,128)(2,1)S(1)} %get-tuple-element.75), channel_id=1, source_target_pairs={{0,24},{2,26},{4,28},{6,30},{8,16},{10,18},{12,20},{14,22},{16,8},... | collective-permute-start | bytes 196616 | tf_op jit(solution)/shard_map/ppermute | solution.py:142
  128.4 1.0 collective-permute-start.19
  129.3 2.8 %collective-permute-done.24 = bf16[4,32,1024]{2,1,0:T(8,128)(2,1)S(1)} collective-permute-done((bf16[4,32,1024]{2,1,0:T(8,128)(2,1)S(1)}, bf16[4,32,1024]{2,1,0:T(8,128)(2,1)S(1)}, u32[]{:S(2)}, u32[]{:S(2)}) %collective-permute-start.24) | collective-permute-done | bytes 262176 | tf_op jit(solution)/shard_map/ppermute | solution.py:142
  132.1 1.4 collective-permute-done.23
  133.5 0.2 fusion.74
  133.7 0.5 collective-permute-start.25
  134.2 2.6 %collective-permute-start.27 = (bf16[1,32,1024]{2,1,0:T(8,128)(2,1)S(1)}, bf16[1,32,1024]{2,1,0:T(8,128)(2,1)S(1)}, u32[]{:S(2)}, u32[]{:S(2)}) collective-permute-start(bf16[1,32,1024]{2,1,0:T(8,128)(2,1)S(1)} %get-tuple-element.78), channel_id=1, source_target_pairs={{0,24},{2,26},{4,28},{6,30},{8,16},{10,18},{12,20},{14,22},{16,8},... | collective-permute-start | bytes 196616 | tf_op jit(solution)/shard_map/ppermute | solution.py:142
  136.8 0.5 collective-permute-start.26
  137.3 1.1 collective-permute-done.25
  138.4 1.8 %collective-permute-done.27 = bf16[1,32,1024]{2,1,0:T(8,128)(2,1)S(1)} collective-permute-done((bf16[1,32,1024]{2,1,0:T(8,128)(2,1)S(1)}, bf16[1,32,1024]{2,1,0:T(8,128)(2,1)S(1)}, u32[]{:S(2)}, u32[]{:S(2)}) %collective-permute-start.27) | collective-permute-done | bytes 65568 | tf_op jit(solution)/shard_map/ppermute | solution.py:142
  140.2 2.4 %collective-permute-done.26 = bf16[1,32,1024]{2,1,0:T(8,128)(2,1)S(1)} collective-permute-done((bf16[1,32,1024]{2,1,0:T(8,128)(2,1)S(1)}, bf16[1,32,1024]{2,1,0:T(8,128)(2,1)S(1)}, u32[]{:S(2)}, u32[]{:S(2)}) %collective-permute-start.26) | collective-permute-done | bytes 65568 | tf_op jit(solution)/shard_map/ppermute | solution.py:142
  142.7 1.0 pad_maximum_fusion
  (60 shorter events, 2.5 us)
Async XLA Ops:
  13.7 2.0 %copy-start.1 = (bf16[32,256,256]{2,1,0:T(8,128)(2,1)}, bf16[32,256,256]{2,1,0:T(8,128)(2,1)S(1)}, u32[]{:S(2)}) copy-start(bf16[32,256,256]{2,1,0:T(8,128)(2,1)S(1)} %get-tuple-element.21.band_ref) | copy-start | bytes 12582916
  15.7 2.2 %copy-start = (bf16[4,1,16,8,4096]{4,3,2,1,0:T(8,128)(2,1)S(1)}, bf16[4,1,16,8,4096]{4,3,2,1,0:T(8,128)(2,1)}, u32[]{:S(2)}) copy-start(bf16[4,1,16,8,4096]{4,3,2,1,0:T(8,128)(2,1)} %param.11) | copy-start | bytes 12582916
  32.5 15.5 %collective-permute-start.4 = (bf16[16,32,1024]{2,1,0:T(8,128)(2,1)S(1)}, bf16[16,32,1024]{2,1,0:T(8,128)(2,1)S(1)}, u32[]{:S(2)}, u32[]{:S(2)}) collective-permute-start(bf16[16,32,1024]{2,1,0:T(8,128)(2,1)S(1)} %bitcast.53), channel_id=1, source_target_pairs={{0,1},{1,0},{2,3},{3,2},{4,5},{5,4},{6,7},{7,6},{8,9},{9,8},{10,11... | collective-permute-start | bytes 3145736 | tf_op jit(solution)/shard_map/ppermute | solution.py:142
  47.8 2.9 %collective-permute-start = (bf16[16,32,1152]{2,1,0:T(8,128)(2,1)S(1)}, bf16[16,32,1152]{2,1,0:T(8,128)(2,1)S(1)}, u32[]{:S(2)}, u32[]{:S(2)}) collective-permute-start(bf16[16,32,1152]{2,1,0:T(8,128)(2,1)S(1)} %bitcast.50), channel_id=1, source_target_pairs={{0,1},{1,0},{2,3},{3,2},{4,5},{5,4},{6,7},{7,6},{8,9},{9,8},{10,11... | collective-permute-start | bytes 3538952 | tf_op jit(solution)/shard_map/ppermute | solution.py:142
  51.3 18.9 %collective-permute-start.1 = (bf16[4,32,1152]{2,1,0:T(8,128)(2,1)S(1)}, bf16[4,32,1152]{2,1,0:T(8,128)(2,1)S(1)}, u32[]{:S(2)}, u32[]{:S(2)}) collective-permute-start(bf16[4,32,1152]{2,1,0:T(8,128)(2,1)S(1)} %get-tuple-element.56), channel_id=1, source_target_pairs={{0,2},{2,0},{4,6},{6,4},{8,10},{10,8},{12,14},{14,12},{16,18},{18,... | collective-permute-start | bytes 884744 | tf_op jit(solution)/shard_map/ppermute | solution.py:142
  54.0 16.2 %collective-permute-start.3 = (bf16[4,32,1152]{2,1,0:T(8,128)(2,1)S(1)}, bf16[4,32,1152]{2,1,0:T(8,128)(2,1)S(1)}, u32[]{:S(2)}, u32[]{:S(2)}) collective-permute-start(bf16[4,32,1152]{2,1,0:T(8,128)(2,1)S(1)} %get-tuple-element.57), channel_id=1, source_target_pairs={{0,6},{2,4},{4,2},{6,0},{8,14},{10,12},{12,10},{14,8},{16,22},{18,... | collective-permute-start | bytes 884744 | tf_op jit(solution)/shard_map/ppermute | solution.py:142
  55.5 15.0 %collective-permute-start.2 = (bf16[4,32,1152]{2,1,0:T(8,128)(2,1)S(1)}, bf16[4,32,1152]{2,1,0:T(8,128)(2,1)S(1)}, u32[]{:S(2)}, u32[]{:S(2)}) collective-permute-start(bf16[4,32,1152]{2,1,0:T(8,128)(2,1)S(1)} %get-tuple-element.58), channel_id=1, source_target_pairs={{0,4},{2,6},{4,0},{6,2},{8,12},{10,14},{12,8},{14,10},{16,20},{18,... | collective-permute-start | bytes 884744 | tf_op jit(solution)/shard_map/ppermute | solution.py:142
  70.1 37.2 %collective-permute-start.14 = (bf16[16,32,1024]{2,1,0:T(8,128)(2,1)S(1)}, bf16[16,32,1024]{2,1,0:T(8,128)(2,1)S(1)}, u32[]{:S(2)}, u32[]{:S(2)}) collective-permute-start(bf16[16,32,1024]{2,1,0:T(8,128)(2,1)S(1)} %bitcast.51), channel_id=1, source_target_pairs={{0,1},{1,0},{2,3},{3,2},{4,5},{5,4},{6,7},{7,6},{8,9},{9,8},{10,11... | collective-permute-start | bytes 3145736 | tf_op jit(solution)/shard_map/ppermute | solution.py:142
  70.7 23.3 %collective-permute-start.5 = (bf16[1,32,1152]{2,1,0:T(8,128)(2,1)S(1)}, bf16[1,32,1152]{2,1,0:T(8,128)(2,1)S(1)}, u32[]{:S(2)}, u32[]{:S(2)}) collective-permute-start(bf16[1,32,1152]{2,1,0:T(8,128)(2,1)S(1)} %get-tuple-element.68), channel_id=1, source_target_pairs={{0,8},{2,10},{4,12},{6,14},{8,0},{10,2},{12,4},{14,6},{16,24},{18,... | collective-permute-start | bytes 221192 | tf_op jit(solution)/shard_map/ppermute | solution.py:142
  72.8 18.3 %collective-permute-start.8 = (bf16[4,32,1024]{2,1,0:T(8,128)(2,1)S(1)}, bf16[4,32,1024]{2,1,0:T(8,128)(2,1)S(1)}, u32[]{:S(2)}, u32[]{:S(2)}) collective-permute-start(bf16[4,32,1024]{2,1,0:T(8,128)(2,1)S(1)} %get-tuple-element.59), channel_id=1, source_target_pairs={{0,2},{2,0},{4,6},{6,4},{8,10},{10,8},{12,14},{14,12},{16,18},{18,... | collective-permute-start | bytes 786440 | tf_op jit(solution)/shard_map/ppermute | solution.py:142
  74.3 19.3 %collective-permute-start.10 = (bf16[4,32,1024]{2,1,0:T(8,128)(2,1)S(1)}, bf16[4,32,1024]{2,1,0:T(8,128)(2,1)S(1)}, u32[]{:S(2)}, u32[]{:S(2)}) collective-permute-start(bf16[4,32,1024]{2,1,0:T(8,128)(2,1)S(1)} %get-tuple-element.60), channel_id=1, source_target_pairs={{0,6},{2,4},{4,2},{6,0},{8,14},{10,12},{12,10},{14,8},{16,22},{18,... | collective-permute-start | bytes 786440 | tf_op jit(solution)/shard_map/ppermute | solution.py:142
  75.8 18.0 %collective-permute-start.9 = (bf16[4,32,1024]{2,1,0:T(8,128)(2,1)S(1)}, bf16[4,32,1024]{2,1,0:T(8,128)(2,1)S(1)}, u32[]{:S(2)}, u32[]{:S(2)}) collective-permute-start(bf16[4,32,1024]{2,1,0:T(8,128)(2,1)S(1)} %get-tuple-element.61), channel_id=1, source_target_pairs={{0,4},{2,6},{4,0},{6,2},{8,12},{10,14},{12,8},{14,10},{16,20},{18,... | collective-permute-start | bytes 786440 | tf_op jit(solution)/shard_map/ppermute | solution.py:142
  91.1 7.0 %collective-permute-start.7 = (bf16[1,32,1152]{2,1,0:T(8,128)(2,1)S(1)}, bf16[1,32,1152]{2,1,0:T(8,128)(2,1)S(1)}, u32[]{:S(2)}, u32[]{:S(2)}) collective-permute-start(bf16[1,32,1152]{2,1,0:T(8,128)(2,1)S(1)} %get-tuple-element.69), channel_id=1, source_target_pairs={{0,24},{2,26},{4,28},{6,30},{8,16},{10,18},{12,20},{14,22},{16,8},... | collective-permute-start | bytes 221192 | tf_op jit(solution)/shard_map/ppermute | solution.py:142
  93.7 7.9 %collective-permute-start.6 = (bf16[1,32,1152]{2,1,0:T(8,128)(2,1)S(1)}, bf16[1,32,1152]{2,1,0:T(8,128)(2,1)S(1)}, u32[]{:S(2)}, u32[]{:S(2)}) collective-permute-start(bf16[1,32,1152]{2,1,0:T(8,128)(2,1)S(1)} %get-tuple-element.70), channel_id=1, source_target_pairs={{0,16},{2,18},{4,20},{6,22},{8,24},{10,26},{12,28},{14,30},{16,0},... | collective-permute-start | bytes 221192 | tf_op jit(solution)/shard_map/ppermute | solution.py:142
  93.9 17.6 %collective-permute-start.21 = (bf16[16,32,1024]{2,1,0:T(8,128)(2,1)S(1)}, bf16[16,32,1024]{2,1,0:T(8,128)(2,1)S(1)}, u32[]{:S(2)}, u32[]{:S(2)}) collective-permute-start(bf16[16,32,1024]{2,1,0:T(8,128)(2,1)S(1)} %bitcast.52), channel_id=1, source_target_pairs={{0,1},{1,0},{2,3},{3,2},{4,5},{5,4},{6,7},{7,6},{8,9},{9,8},{10,11... | collective-permute-start | bytes 3145736 | tf_op jit(solution)/shard_map/ppermute | solution.py:142
  94.1 7.5 %collective-permute-start.11 = (bf16[1,32,1024]{2,1,0:T(8,128)(2,1)S(1)}, bf16[1,32,1024]{2,1,0:T(8,128)(2,1)S(1)}, u32[]{:S(2)}, u32[]{:S(2)}) collective-permute-start(bf16[1,32,1024]{2,1,0:T(8,128)(2,1)S(1)} %get-tuple-element.71), channel_id=1, source_target_pairs={{0,8},{2,10},{4,12},{6,14},{8,0},{10,2},{12,4},{14,6},{16,24},{18,... | collective-permute-start | bytes 196616 | tf_op jit(solution)/shard_map/ppermute | solution.py:142
  98.1 6.1 %collective-permute-start.13 = (bf16[1,32,1024]{2,1,0:T(8,128)(2,1)S(1)}, bf16[1,32,1024]{2,1,0:T(8,128)(2,1)S(1)}, u32[]{:S(2)}, u32[]{:S(2)}) collective-permute-start(bf16[1,32,1024]{2,1,0:T(8,128)(2,1)S(1)} %get-tuple-element.72), channel_id=1, source_target_pairs={{0,24},{2,26},{4,28},{6,30},{8,16},{10,18},{12,20},{14,22},{16,8},... | collective-permute-start | bytes 196616 | tf_op jit(solution)/shard_map/ppermute | solution.py:142
  101.5 5.8 %collective-permute-start.12 = (bf16[1,32,1024]{2,1,0:T(8,128)(2,1)S(1)}, bf16[1,32,1024]{2,1,0:T(8,128)(2,1)S(1)}, u32[]{:S(2)}, u32[]{:S(2)}) collective-permute-start(bf16[1,32,1024]{2,1,0:T(8,128)(2,1)S(1)} %get-tuple-element.73), channel_id=1, source_target_pairs={{0,16},{2,18},{4,20},{6,22},{8,24},{10,26},{12,28},{14,30},{16,0},... | collective-permute-start | bytes 196616 | tf_op jit(solution)/shard_map/ppermute | solution.py:142
  107.9 9.3 %collective-permute-start.15 = (bf16[4,32,1024]{2,1,0:T(8,128)(2,1)S(1)}, bf16[4,32,1024]{2,1,0:T(8,128)(2,1)S(1)}, u32[]{:S(2)}, u32[]{:S(2)}) collective-permute-start(bf16[4,32,1024]{2,1,0:T(8,128)(2,1)S(1)} %get-tuple-element.62), channel_id=1, source_target_pairs={{0,2},{2,0},{4,6},{6,4},{8,10},{10,8},{12,14},{14,12},{16,18},{18,... | collective-permute-start | bytes 786440 | tf_op jit(solution)/shard_map/ppermute | solution.py:142
  109.2 14.3 %collective-permute-start.17 = (bf16[4,32,1024]{2,1,0:T(8,128)(2,1)S(1)}, bf16[4,32,1024]{2,1,0:T(8,128)(2,1)S(1)}, u32[]{:S(2)}, u32[]{:S(2)}) collective-permute-start(bf16[4,32,1024]{2,1,0:T(8,128)(2,1)S(1)} %get-tuple-element.63), channel_id=1, source_target_pairs={{0,6},{2,4},{4,2},{6,0},{8,14},{10,12},{12,10},{14,8},{16,22},{18,... | collective-permute-start | bytes 786440 | tf_op jit(solution)/shard_map/ppermute | solution.py:142
  110.7 14.9 %collective-permute-start.16 = (bf16[4,32,1024]{2,1,0:T(8,128)(2,1)S(1)}, bf16[4,32,1024]{2,1,0:T(8,128)(2,1)S(1)}, u32[]{:S(2)}, u32[]{:S(2)}) collective-permute-start(bf16[4,32,1024]{2,1,0:T(8,128)(2,1)S(1)} %get-tuple-element.64), channel_id=1, source_target_pairs={{0,4},{2,6},{4,0},{6,2},{8,12},{10,14},{12,8},{14,10},{16,20},{18,... | collective-permute-start | bytes 786440 | tf_op jit(solution)/shard_map/ppermute | solution.py:142
  112.0 16.4 %collective-permute-start.22 = (bf16[4,32,1024]{2,1,0:T(8,128)(2,1)S(1)}, bf16[4,32,1024]{2,1,0:T(8,128)(2,1)S(1)}, u32[]{:S(2)}, u32[]{:S(2)}) collective-permute-start(bf16[4,32,1024]{2,1,0:T(8,128)(2,1)S(1)} %get-tuple-element.65), channel_id=1, source_target_pairs={{0,2},{2,0},{4,6},{6,4},{8,10},{10,8},{12,14},{14,12},{16,18},{18,... | collective-permute-start | bytes 786440 | tf_op jit(solution)/shard_map/ppermute | solution.py:142
  113.3 18.8 %collective-permute-start.24 = (bf16[4,32,1024]{2,1,0:T(8,128)(2,1)S(1)}, bf16[4,32,1024]{2,1,0:T(8,128)(2,1)S(1)}, u32[]{:S(2)}, u32[]{:S(2)}) collective-permute-start(bf16[4,32,1024]{2,1,0:T(8,128)(2,1)S(1)} %get-tuple-element.66), channel_id=1, source_target_pairs={{0,6},{2,4},{4,2},{6,0},{8,14},{10,12},{12,10},{14,8},{16,22},{18,... | collective-permute-start | bytes 786440 | tf_op jit(solution)/shard_map/ppermute | solution.py:142
  117.2 16.4 %collective-permute-start.23 = (bf16[4,32,1024]{2,1,0:T(8,128)(2,1)S(1)}, bf16[4,32,1024]{2,1,0:T(8,128)(2,1)S(1)}, u32[]{:S(2)}, u32[]{:S(2)}) collective-permute-start(bf16[4,32,1024]{2,1,0:T(8,128)(2,1)S(1)} %get-tuple-element.67), channel_id=1, source_target_pairs={{0,4},{2,6},{4,0},{6,2},{8,12},{10,14},{12,8},{14,10},{16,20},{18,... | collective-permute-start | bytes 786440 | tf_op jit(solution)/shard_map/ppermute | solution.py:142
  125.8 11.0 %collective-permute-start.18 = (bf16[1,32,1024]{2,1,0:T(8,128)(2,1)S(1)}, bf16[1,32,1024]{2,1,0:T(8,128)(2,1)S(1)}, u32[]{:S(2)}, u32[]{:S(2)}) collective-permute-start(bf16[1,32,1024]{2,1,0:T(8,128)(2,1)S(1)} %get-tuple-element.74), channel_id=1, source_target_pairs={{0,8},{2,10},{4,12},{6,14},{8,0},{10,2},{12,4},{14,6},{16,24},{18,... | collective-permute-start | bytes 196616 | tf_op jit(solution)/shard_map/ppermute | solution.py:142
  126.1 11.2 %collective-permute-start.20 = (bf16[1,32,1024]{2,1,0:T(8,128)(2,1)S(1)}, bf16[1,32,1024]{2,1,0:T(8,128)(2,1)S(1)}, u32[]{:S(2)}, u32[]{:S(2)}) collective-permute-start(bf16[1,32,1024]{2,1,0:T(8,128)(2,1)S(1)} %get-tuple-element.75), channel_id=1, source_target_pairs={{0,24},{2,26},{4,28},{6,30},{8,16},{10,18},{12,20},{14,22},{16,8},... | collective-permute-start | bytes 196616 | tf_op jit(solution)/shard_map/ppermute | solution.py:142
  128.4 8.9 %collective-permute-start.19 = (bf16[1,32,1024]{2,1,0:T(8,128)(2,1)S(1)}, bf16[1,32,1024]{2,1,0:T(8,128)(2,1)S(1)}, u32[]{:S(2)}, u32[]{:S(2)}) collective-permute-start(bf16[1,32,1024]{2,1,0:T(8,128)(2,1)S(1)} %get-tuple-element.76), channel_id=1, source_target_pairs={{0,16},{2,18},{4,20},{6,22},{8,24},{10,26},{12,28},{14,30},{16,0},... | collective-permute-start | bytes 196616 | tf_op jit(solution)/shard_map/ppermute | solution.py:142
  133.7 4.7 %collective-permute-start.25 = (bf16[1,32,1024]{2,1,0:T(8,128)(2,1)S(1)}, bf16[1,32,1024]{2,1,0:T(8,128)(2,1)S(1)}, u32[]{:S(2)}, u32[]{:S(2)}) collective-permute-start(bf16[1,32,1024]{2,1,0:T(8,128)(2,1)S(1)} %get-tuple-element.77), channel_id=1, source_target_pairs={{0,8},{2,10},{4,12},{6,14},{8,0},{10,2},{12,4},{14,6},{16,24},{18,... | collective-permute-start | bytes 196616 | tf_op jit(solution)/shard_map/ppermute | solution.py:142
  134.2 6.1 %collective-permute-start.27 = (bf16[1,32,1024]{2,1,0:T(8,128)(2,1)S(1)}, bf16[1,32,1024]{2,1,0:T(8,128)(2,1)S(1)}, u32[]{:S(2)}, u32[]{:S(2)}) collective-permute-start(bf16[1,32,1024]{2,1,0:T(8,128)(2,1)S(1)} %get-tuple-element.78), channel_id=1, source_target_pairs={{0,24},{2,26},{4,28},{6,30},{8,16},{10,18},{12,20},{14,22},{16,8},... | collective-permute-start | bytes 196616 | tf_op jit(solution)/shard_map/ppermute | solution.py:142
  136.8 5.9 %collective-permute-start.26 = (bf16[1,32,1024]{2,1,0:T(8,128)(2,1)S(1)}, bf16[1,32,1024]{2,1,0:T(8,128)(2,1)S(1)}, u32[]{:S(2)}, u32[]{:S(2)}) collective-permute-start(bf16[1,32,1024]{2,1,0:T(8,128)(2,1)S(1)} %get-tuple-element.79), channel_id=1, source_target_pairs={{0,16},{2,18},{4,20},{6,22},{8,24},{10,26},{12,28},{14,30},{16,0},... | collective-permute-start | bytes 196616 | tf_op jit(solution)/shard_map/ppermute | solution.py:142

commit v2 on v1

--- a/solution.py
+++ b/solution.py
@@ -11,9 +11,9 @@
 SLAB_ROWS = 64
 ROWS = 8
 TAPS_OUT = 36
-CHUNKS = 4
+BLOCKS = 3
 EMPTY = 128
-VMEM_LIMIT = 42 * 1024 * 1024
+VMEM_LIMIT = 58 * 1024 * 1024
 HI = lax.Precision.HIGHEST
 
 
@@ -82,70 +82,151 @@
     lax.fori_loop(0, patches, one_patch, 0)
 
 
-def field_sizes(bits):
-    sizes = [2] * (bits // 2)
-    return sizes + [1] * (bits % 2)
-
-
-def main_kernel(first_block, blocks, patch_bits, streams, strip_ref, x_ref, band_ref, w_ref, keep_ref, send_ref, f_ref):
+def partner(me, mask):
+    other, bit = me, 1
+    while bit <= mask:
+        if mask & bit:
+            other = other + bit * (1 - 2 * ((me // bit) % 2))
+        bit *= 2
+    return other
+
+
+def fused_kernel(
+    strip_ref, x_ref, band_ref, w_ref, out_ref,
+    f_ref, keep0, keep1, keep2, out0, out1, out2, in0, in1, in2, *sems
+):
     steps = x_ref.shape[0]
     strips = x_ref.shape[1] // ROWS
-    tiles = x_ref.shape[2] // 128
     patches = w_ref.shape[0]
-    part = SLAB_ROWS // streams
-    width = blocks * 128
-
-    def one_step(t, c):
-        pieces = []
-        for n in range(first_block, first_block + blocks):
-            if 0 <= n and n + 2 <= tiles:
-                pieces.append(x_ref[t, :, n * 128 : n * 128 + 256])
-            else:
-                blank = jnp.zeros((strips * ROWS, 128), jnp.bfloat16)
-                sides = [x_ref[t, :, m * 128 : (m + 1) * 128] if 0 <= m < tiles else blank for m in (n, n + 1)]
-                pieces.append(jnp.concatenate(sides, axis=1))
-        lhs = jnp.concatenate(pieces, axis=0)
-        for g in range(8):
-            res = jnp.dot(lhs, band_ref[t * 8 + g], preferred_element_type=jnp.float32)
-            res = res.reshape(blocks, strips, ROWS, 256)
-            for n in range(blocks):
-                two = jnp.concatenate([res[n, :, :, :128], res[n, :, :, 128:]], axis=1)
-                f_ref[pl.ds(t * strips, strips), g, :, n * 128 : (n + 1) * 128] = two.astype(jnp.bfloat16)
-        return c
-
-    lax.fori_loop(0, steps, one_step, 0)
-
-    def one_patch(q):
-        rhs = jnp.concatenate(
-            [f_ref[strip_ref[q * steps * 2 + k]].reshape(128, width) for k in range(2 * steps)], axis=0
+    chunks, part, width = out_ref.shape
+    streams = SLAB_ROWS // part
+    fields = [1 << 2, patches >> 2]
+    my_patch, my_stream = lax.axis_index("patch"), lax.axis_index("stream")
+    peers = [
+        [{"stream": partner(my_stream, g)} for g in range(1, streams)],
+        [{"patch": partner(my_patch, g)} for g in range(1, fields[0])],
+        [{"patch": partner(my_patch, g * fields[0])} for g in range(1, fields[1])],
+    ]
+    outs, ins = (out0, out1, out2), (in0, in1, in2)
+    gone, come = sems[:3], sems[3:]
+
+    barrier = pltpu.get_barrier_semaphore()
+    for group in peers:
+        for device in group:
+            pl.semaphore_signal(barrier, inc=1, device_id=device, device_id_type=pl.DeviceIdType.MESH)
+    pl.semaphore_wait(barrier, sum(len(group) for group in peers))
+
+    def copy(k, c, g):
+        return pltpu.make_async_remote_copy(
+            src_ref=outs[k].at[c, g],
+            dst_ref=ins[k].at[c, g],
+            send_sem=gone[k].at[c, g],
+            recv_sem=come[k].at[c, g],
+            device_id=peers[k][g],
+            device_id_type=pl.DeviceIdType.MESH,
         )
-        acc = jnp.dot(w_ref[q], rhs, preferred_element_type=jnp.float32)
-        pos, low, left = 0, 0, patches
-        for size in field_sizes(patch_bits):
-            left = left >> size
-            pos = pos + (lax.shift_right_logical(q, low) & ((1 << size) - 1)) * left
-            low += size
-        keep_ref[pos] = acc[:part]
-        for s in range(1, streams):
-            send_ref[s - 1, pos] = acc[s * part : (s + 1) * part].astype(jnp.bfloat16)
-
-    def four(i, c):
-        for k in range(4):
-            one_patch(i * 4 + k)
-        return c
-
-    lax.fori_loop(0, patches // 4, four, 0)
-
-
-def swap(x, axis, mask):
-    n = lax.axis_size(axis)
-    return lax.ppermute(x, axis, [(i, i ^ mask) for i in range(n)])
-
-
-def add_all(keep, arrived):
-    for one in arrived:
-        keep = keep + one.astype(jnp.float32)
-    return keep
+
+    def compute(c):
+        def one_step(t, carry):
+            pieces = [
+                x_ref[t, :, pl.ds(pl.multiple_of((c * BLOCKS + n) * 128, 128), 256)] for n in range(BLOCKS)
+            ]
+            lhs = jnp.concatenate(pieces, axis=0)
+            for g in range(8):
+                res = jnp.dot(lhs, band_ref[t * 8 + g], preferred_element_type=jnp.float32)
+                res = res.reshape(BLOCKS, strips, ROWS, 256)
+                for n in range(BLOCKS):
+                    two = jnp.concatenate([res[n, :, :, :128], res[n, :, :, 128:]], axis=1)
+                    f_ref[pl.ds(t * strips, strips), g, :, n * 128 : (n + 1) * 128] = two.astype(jnp.bfloat16)
+            return carry
+
+        lax.fori_loop(0, steps, one_step, 0)
+
+        def four(i, carry):
+            for k in range(fields[0]):
+                q = i * fields[0] + k
+                rhs = jnp.concatenate(
+                    [f_ref[strip_ref[q * steps * 2 + m]].reshape(128, width) for m in range(2 * steps)], axis=0
+                )
+                acc = jnp.dot(w_ref[q], rhs, preferred_element_type=jnp.float32)
+                pos = k * fields[1] + i
+                keep0[c % 2, pos] = acc[:part]
+                for s in range(1, streams):
+                    out0[c, s - 1, pos] = acc[s * part : (s + 1) * part].astype(jnp.bfloat16)
+            return carry
+
+        lax.fori_loop(0, fields[1], four, 0)
+
+    def arrive(k, c):
+        for g in range(len(peers[k])):
+            copy(k, c, g).wait_recv()
+
+    def send(k, c):
+        for g in range(len(peers[k])):
+            copy(k, c, g).start()
+
+    def slot(i, carry):
+        @pl.when(i < chunks)
+        def _():
+            compute(i)
+            send(0, i)
+
+        @pl.when(i >= 3)
+        def _():
+            c = i - 3
+            arrive(2, c)
+            total = keep2[...]
+            for g in range(len(peers[2])):
+                total = total + in2[c, g, 0].astype(jnp.float32)
+            out_ref[c] = total
+
+        @pl.when((i >= 2) & (i < chunks + 2))
+        def _():
+            c = i - 2
+            arrive(1, c)
+
+            def one(z):
+                total = keep1[z]
+                for g in range(len(peers[1])):
+                    total = total + in1[c, g, z].astype(jnp.float32)
+                return total
+
+            keep2[...] = one(0)
+            for z in range(1, fields[1]):
+                out2[c, z - 1, 0] = one(z).astype(jnp.bfloat16)
+            send(2, c)
+
+        @pl.when((i >= 1) & (i < chunks + 1))
+        def _():
+            c = i - 1
+            arrive(0, c)
+
+            def one(z, carry):
+                for k in range(fields[0]):
+                    pos = k * fields[1] + z
+                    total = keep0[c % 2, pos]
+                    for g in range(len(peers[0])):
+                        total = total + in0[c, g, pos].astype(jnp.float32)
+                    if k == 0:
+                        keep1[z] = total
+                    else:
+                        out1[c, k - 1, z] = total.astype(jnp.bfloat16)
+                return carry
+
+            lax.fori_loop(0, fields[1], one, 0)
+            send(1, c)
+
+        return carry
+
+    lax.fori_loop(0, chunks + 3, slot, 0)
+
+    def leave(c, carry):
+        for k in range(3):
+            for g in range(len(peers[k])):
+                copy(k, c, g).wait_send()
+        return carry
+
+    lax.fori_loop(0, chunks, leave, 0)
 
 
 def shards(
@@ -157,9 +238,11 @@
     my_stream = lax.axis_index("stream")
     steps, strips, width = exposures.shape[0], exposures.shape[2], exposures.shape[4]
     part = SLAB_ROWS // streams
-    patch_bits = patches.bit_length() - 1
-
-    x = exposures.reshape(steps, strips * ROWS, width)
+    chunks = -(-(width // 128 + 1) // BLOCKS)
+    wide = BLOCKS * 128
+    padded = chunks * wide - width
+
+    x = jnp.pad(exposures.reshape(steps, strips * ROWS, width), ((0, 0), (0, 0), (128, padded)))
 
     warp = lanczos_taps(visit_shift[:, 0])
     vrows = column_rows(basis_x, warp[:, 0]).reshape(-1, 256)
@@ -198,43 +281,32 @@
         compiler_params=params,
     )(start, my_stream.reshape(1).astype(jnp.int32), vrows, k2)
 
-    total_blocks = width // 128 + 1
-    sizes = [total_blocks // CHUNKS + (c < total_blocks % CHUNKS) for c in range(CHUNKS)]
-    fields = field_sizes(patch_bits)
-
-    def hop(total, k):
-        low = sum(fields[:k])
-        parts = total.reshape(1 << fields[k], -1, part, total.shape[-1])
-        sends = [parts[g].astype(jnp.bfloat16) for g in range(1, 1 << fields[k])]
-        return add_all(parts[0], [swap(v, "patch", (g + 1) << low) for g, v in enumerate(sends)])
-
-    sums = []
-    begin = -1
-    for c, blocks in enumerate(sizes):
-        wide = blocks * 128
-        table = strip
-        if c >= 2:
-            table, *tied = lax.optimization_barrier((strip, *sums[max(0, c - 1 - len(fields)) : c - 1]))
-            for k, total in enumerate(reversed(tied)):
-                sums[c - 2 - k] = hop(total, k)
-        keep, send = pl.pallas_call(
-            functools.partial(main_kernel, begin, blocks, patch_bits, streams),
-            in_specs=[smem, vmem, vmem, vmem],
-            out_specs=(vmem, vmem),
-            out_shape=(
-                jax.ShapeDtypeStruct((patches, part, wide), jnp.float32),
-                jax.ShapeDtypeStruct((streams - 1, patches, part, wide), jnp.bfloat16),
-            ),
-            scratch_shapes=[pltpu.VMEM((steps * strips, 8, 16, wide), jnp.bfloat16)],
-            compiler_params=params,
-            cost_estimate=pl.CostEstimate(flops=12 << 30, bytes_accessed=12 << 20, transcendentals=0),
-        )(table, x, band, w)
-        begin += blocks
-        sums.append(add_all(keep, [swap(send[s - 1], "stream", s) for s in range(1, streams)]))
-    for c in range(CHUNKS):
-        for k in range(min(len(fields), max(0, CHUNKS - 2 - c + 0)), len(fields)):
-            sums[c] = hop(sums[c], k)
-    out = jnp.concatenate([total[0] for total in sums], axis=1)
+    near, far = 4, patches // 4
+    bf16, f32 = jnp.bfloat16, jnp.float32
+    shapes = [(streams - 1, patches), (near - 1, far), (far - 1, 1)]
+    buffers = [pltpu.VMEM((chunks, n, m, part, wide), bf16) for n, m in shapes]
+    sems = [pltpu.SemaphoreType.DMA((chunks, n)) for n, m in shapes]
+    out = pl.pallas_call(
+        fused_kernel,
+        in_specs=[smem, vmem, vmem, vmem],
+        out_specs=vmem,
+        out_shape=jax.ShapeDtypeStruct((chunks, part, wide), f32),
+        scratch_shapes=[
+            pltpu.VMEM((steps * strips, 8, 16, wide), bf16),
+            pltpu.VMEM((2, patches, part, wide), f32),
+            pltpu.VMEM((far, part, wide), f32),
+            pltpu.VMEM((part, wide), f32),
+            *buffers,
+            *buffers,
+            *sems,
+            *sems,
+        ],
+        compiler_params=pltpu.CompilerParams(
+            vmem_limit_bytes=VMEM_LIMIT, collective_id=0, has_side_effects=True
+        ),
+        cost_estimate=pl.CostEstimate(flops=30 << 30, bytes_accessed=12 << 20, transcendentals=0),
+    )(strip, x, band, w)
+    out = out.transpose(1, 0, 2).reshape(part, chunks * wide)
     return out[:, 96 : 96 + width]
 
 

time: 144 us -> 117 us (0.81)
  Pallas kernels: 63.2 us -> 98.4 us
  waiting for transfers between devices: 31.4 us -> 0 us
  starting transfers between devices: 31.3 us -> 0 us
  local copies, waits for them, and re-layouts: 5.76 us -> 9.69 us
  other arithmetic: 11.6 us -> 8.61 us
    pallas_call x4 -> x1, Pallas kernels: 58.8 us -> 90.8 us  [shards(): pl.pallas_call(fused_kernel, in_specs=[smem, vmem, vmem, vmem], out_specs...]
    ppermute x28 -> x0, waiting for transfers between devices: 31.4 us -> none  [swap(): return lax.ppermute(x, axis, [(i, i ^ mask) for i in range(n)])]
    ppermute x28 -> x0, starting transfers between devices: 31.3 us -> none  [swap(): return lax.ppermute(x, axis, [(i, i ^ mask) for i in range(n)])]
    pad x0 -> x1, local copies, waits for them, and re-layouts: none -> 4.54 us  [shards(): jnp.pad(exposures.reshape(steps, strips * ROWS, width), ((0, 0), (0, 0),...]
    unnamed x4 -> x0, local copies, waits for them, and re-layouts: 4.14 us -> none
    pallas_call x1, Pallas kernels: 4.4 us -> 7.58 us  [shards(): pl.pallas_call(functools.partial(prep_kernel, streams), out_shape=(jax.Sh...]
    another operation x8 -> x0, other arithmetic: 1.71 us -> none
  transfers between devices with their start and end apart: 28 -> 0, of which waited for: 14 -> 0; matrix products, arithmetic and copies ran while one was open for 2% -> 0% of each run, Pallas kernels for 31% -> 0%
where the time goes in v2:
time: 117 us
  Pallas kernels  98.4 us (84%)
  local copies, waits for them, and re-layouts  9.69 us (8%)
  other arithmetic  8.61 us (7%)
    pallas_call x1, Pallas kernels, shards(): pl.pallas_call(fused_kernel, in_specs=[smem, vmem, vmem, vmem], out_specs...  90.8 us
    pallas_call x1, Pallas kernels, shards(): pl.pallas_call(functools.partial(prep_kernel, streams), out_shape=(jax.Sh...  7.58 us
    pad x1, local copies, waits for them, and re-layouts, shards(): jnp.pad(exposures.reshape(steps, strips * ROWS, width), ((0, 0), (0, 0),...  4.54 us

profile of v2, /device:TPU:0, one launch (start us, length us, event | category | flops | bytes accessed | tf_op | source)
XLA Modules:
  0.0 116.7 jit_solution(11154213756876964136)
XLA Ops:
  0.0 0.7 fusion.44
  0.7 0.8 multiply_reduce_fusion.1
  1.5 0.7 broadcast_multiply_fusion.6
  2.2 0.9 fusion.41
  3.1 0.3 slice_reduce_fusion.5
  3.4 0.8 multiply_reduce_fusion
  4.2 0.8 compare_reduce_fusion
  5.0 0.2 select_reduce_fusion.3
  5.2 0.1 bitcast_add_fusion.1
  5.3 0.1 copy.41
  5.4 0.7 reshape.187.strip_ref
  6.1 0.8 fusion.5
  6.9 0.1 rev.7
  7.0 0.8 fusion
  7.8 0.3 select_reduce_fusion.1
  8.1 0.1 copy.44
  8.2 0.7 reshape.189.starts_ref
  8.9 0.8 broadcast_multiply_fusion.5
  9.7 0.1 fusion.4
  9.8 0.1 rev.6
  9.9 0.7 pad.71
  10.6 0.1 copy.45
  10.7 0.1 tile.10
  10.9 0.9 multiply_add_fusion.k2_ref
  11.8 4.5 %pad.64.x_ref = bf16[4,128,4352]{2,1,0:T(8,128)(2,1)} pad(bf16[4,128,4096]{2,1,0:T(8,128)(2,1)} %bitcast.36, bf16[]{:T(256)} %constant.63.clone.1), padding=0_0x0_0x128_128 | pad | bytes 8650754 | tf_op jit(solution)/shard_map/jit(_pad)/pad | solution.py:245
  16.3 7.6 %shard_map.106 = (bf16[32,256,256]{2,1,0:T(8,128)(2,1)}, bf16[16,64,1024]{2,1,0:T(8,128)(2,1)}) custom-call(s32[128]{0:T(128)} %reshape.189.starts_ref, s32[1]{0:T(128)} %bitcast.7.me_ref, f32[64,256]{1,0:T(8,128)} %bitcast.39, f32[4,192,128]{2,1,0:T(8,128)} %multiply_add_fusion.k2_ref), custom_call_target="tpu_custom_call" | custom-call | tf_op jit(solution)/shard_map/pallas_call | solution.py:273
  23.9 90.8 %shard_map.107 = f32[11,32,384]{2,1,0:T(8,128)} custom-call(s32[128]{0:T(128)} %reshape.187.strip_ref, bf16[4,128,4352]{2,1,0:T(8,128)(2,1)} %pad.64.x_ref, bf16[32,256,256]{2,1,0:T(8,128)(2,1)} %get-tuple-element.8.band_ref, bf16[16,64,1024]{2,1,0:T(8,128)(2,1)} %get-tuple-element.9.w_ref), custom_call_target="tpu_custom_call" | custom-call | flops 32212254720 | bytes 12582912 | tf_op jit(solution)/shard_map/pallas_call | solution.py:289
  114.7 1.1 copy.56
  115.7 1.0 slice.78
  (11 shorter events, 0.1 us)
